TPU v7x, 32 devices: a whole 2x2x4 slice. The times are simulated.
32 devices in a mesh: gx: 8 (over y, x, core), gy: 4 (over z).
Axes of the slice: x: 2, y: 2, z: 4, core: 2. Of those that a mesh axis runs over, the one named last changes fastest.
Arguments:
- velocity: float32 [3, 128, 64, 512], P(None, 'gx', 'gy'), may hold values from -6 to 6
- stress: float32 [6, 128, 64, 512], P(None, 'gx', 'gy'), may hold values from -6 to 6
- pier_velocity: float32 [128, 16], P('gx', 'gy'), may hold values from -6 to 6
- buoyancy: float32 [128, 64, 512], P('gx', 'gy'), may hold values from 0.5 to 2
- layer: int32 [128], P('gx'), may hold values from 0 to 7, as said below
- lame_table: float32 [8], replicated, may hold values from 0.3 to 1.2
- shear_table: float32 [8], replicated, may hold values from 0.2 to 0.8
- relax_table: float32 [8], replicated, may hold values from 0.6 to 0.95
- impedance: float32 [16], P('gy'), may hold values from 0.5 to 2
- footprint: int32 [16, 16], replicated, may hold values from 0 to 32767, as said below
- damp_inverse: float32 [128, 128], replicated
Outputs:
- velocity_out: float32 [3, 128, 64, 512], P(None, 'gx', 'gy')
- stress_out: float32 [6, 128, 64, 512], P(None, 'gx', 'gy')
- pier_out: float32 [128, 16], P('gx', 'gy')
Inputs may be any that keep to these rules, and one draw needn't show every extreme that they name: `footprint`: row p lists the 16 cells of a square of 4 by 4 cells, row by row; squares may intersect and lie anywhere in the plane. `layer`: non-decreasing along depth; the first cell is in layer 0 and the last in layer 7.
All inputs are finite; a program needn't handle non-finite values.
Results may differ from a plain program's by a relative error of at most 0.00011.
Values sent between devices are 32-bit elements; how exact they have to be, the bound alone decides.
A program may use at most 192 MiB of HBM per device.

v0:
```python
import jax
import jax.numpy as jnp
from jax import lax
from jax.sharding import PartitionSpec as P

STEPS = 2
FOOT = 16


grid_ratio = 0.25
soil_gain = 0.2
pier_gain = 0.5


def extended(cells, sides, width):
    for axis, dim in sides:
        count = lax.axis_size(axis)
        ends = count - 1
        head = lax.slice_in_dim(cells, 0, width, axis=dim)
        tail = lax.slice_in_dim(cells, cells.shape[dim] - width, cells.shape[dim], axis=dim)
        cells = jnp.concatenate(
            [
                lax.ppermute(tail, axis, [(i, (i + 1) % count) for i in range(ends)]),
                cells,
                lax.ppermute(head, axis, [((i + 1) % count, i) for i in range(ends)]),
            ],
            axis=dim,
        )
    return cells


def forward_diff(padded, along):
    center = padded[1:-1, 1:-1, 1:-1]
    if along == 0:
        return padded[2:, 1:-1, 1:-1] - center
    if along == 1:
        return padded[1:-1, 2:, 1:-1] - center
    return padded[1:-1, 1:-1, 2:] - center


def backward_diff(padded, along):
    center = padded[1:-1, 1:-1, 1:-1]
    if along == 0:
        return center - padded[:-2, 1:-1, 1:-1]
    if along == 1:
        return center - padded[1:-1, :-2, 1:-1]
    return center - padded[1:-1, 1:-1, :-2]


def move_velocity(velocity, padded, buoyancy):
    scaled = grid_ratio * buoyancy
    first = velocity[0] + scaled * (
        backward_diff(padded[0], 2) + forward_diff(padded[3], 1) + forward_diff(padded[4], 0)
    )
    second = velocity[1] + scaled * (
        forward_diff(padded[3], 2) + backward_diff(padded[1], 1) + forward_diff(padded[5], 0)
    )
    third = velocity[2] + scaled * (
        forward_diff(padded[4], 2) + forward_diff(padded[5], 1) + backward_diff(padded[2], 0)
    )
    return jnp.stack([first, second, third])


def move_stress(stress, padded, lame_first, shear_mod, relax):
    strain_x = forward_diff(padded[0], 2)
    strain_y = forward_diff(padded[1], 1)
    strain_z = forward_diff(padded[2], 0)
    modulus = lame_first + 2.0 * shear_mod
    normal_x = relax * stress[0] + grid_ratio * (
        modulus * strain_x + lame_first * (strain_y + strain_z)
    )
    normal_y = relax * stress[1] + grid_ratio * (
        modulus * strain_y + lame_first * (strain_x + strain_z)
    )
    normal_z = relax * stress[2] + grid_ratio * (
        modulus * strain_z + lame_first * (strain_x + strain_y)
    )
    shear_xy = relax * stress[3] + grid_ratio * shear_mod * (
        backward_diff(padded[0], 1) + backward_diff(padded[1], 2)
    )
    shear_xz = relax * stress[4] + grid_ratio * shear_mod * (
        backward_diff(padded[0], 0) + backward_diff(padded[2], 2)
    )
    shear_yz = relax * stress[5] + grid_ratio * shear_mod * (
        backward_diff(padded[1], 0) + backward_diff(padded[2], 1)
    )
    return jnp.stack([normal_x, normal_y, normal_z, shear_xy, shear_xz, shear_yz])


def layer_values(layer, table):
    levels = jnp.arange(table.shape[0], dtype=jnp.int32)
    onehot = (layer[:, None] == levels[None, :]).astype(table.dtype)
    return jnp.sum(onehot * table[None, :], axis=1)[:, None, None]


def with_faces(fields):
    padded = extended(fields, (("gx", 1), ("gy", 2)), 1)
    return jnp.pad(padded, ((0, 0), (0, 0), (0, 0), (1, 1)))


def footprint_matches(cell_ids, footprint):
    piers = footprint.shape[0]
    equal = (cell_ids[:, None] == footprint.reshape(-1)[None, :]).astype(jnp.float32)
    return jnp.sum(equal.reshape(cell_ids.shape[0], piers, FOOT), axis=2)


def damp_columns(velocity, inverse):
    pencils = lax.all_to_all(velocity, "gx", split_axis=3, concat_axis=1, tiled=True)
    shape = pencils.shape
    flat = pencils.reshape(shape[0], shape[1], shape[2] * shape[3])
    damped = jnp.einsum("zk,fkm->fzm", inverse, flat, precision=lax.Precision.HIGHEST).reshape(
        shape
    )
    return lax.all_to_all(damped, "gx", split_axis=1, concat_axis=3, tiled=True)


def body(
    velocity,
    stress,
    pier_velocity,
    buoyancy,
    layer,
    lame_table,
    shear_table,
    relax_table,
    impedance,
    footprint,
    damp_inverse,
):
    depth_cells, side_cells, line_cells = (velocity.shape[1], velocity.shape[2], velocity.shape[3])
    own_piers = pier_velocity.shape[1]
    lame_first = layer_values(layer, lame_table)
    shear_mod = layer_values(layer, shear_table)
    relax = layer_values(layer, relax_table)
    row_start = lax.axis_index("gy") * side_cells
    cell_ids = row_start * line_cells + jnp.arange(side_cells * line_cells, dtype=jnp.int32)
    selector = footprint_matches(cell_ids, footprint)
    own_foot = lax.dynamic_slice_in_dim(footprint, lax.axis_index("gy") * own_piers, own_piers, 0)
    for time_step in range(STEPS):
        padded = with_faces(stress)
        velocity = move_velocity(velocity, padded, buoyancy)
        vertical = velocity[2].reshape(depth_cells, side_cells * line_cells)
        piece = lax.all_gather(velocity[2], "gy", axis=1, tiled=True)
        count = piece.shape[1]
        piece_ids = jnp.arange(count * line_cells, dtype=jnp.int32)
        picks = footprint_matches(piece_ids, own_foot)
        flat = piece.reshape(depth_cells, count * line_cells)
        summed = jnp.dot(
            flat, picks, precision=lax.Precision.HIGHEST, preferred_element_type=jnp.float32
        )
        mean_speed = summed / FOOT
        force = impedance[None, :] * (pier_velocity - mean_speed)
        pier_velocity = pier_velocity - pier_gain * force
        all_force = lax.all_gather(force, "gy", axis=1, tiled=True)
        pushed = jnp.dot(
            all_force,
            selector.T,
            precision=lax.Precision.HIGHEST,
            preferred_element_type=jnp.float32,
        )
        vertical = vertical + soil_gain * pushed
        velocity = jnp.stack(
            [velocity[0], velocity[1], vertical.reshape(depth_cells, side_cells, line_cells)]
        )
        velocity = damp_columns(velocity, damp_inverse)
        padded = with_faces(velocity)
        stress = move_stress(stress, padded, lame_first, shear_mod, relax)
    return (velocity, stress, pier_velocity)


def solution(mesh):
    placed = (
        P(None, "gx", "gy", None),
        P(None, "gx", "gy", None),
        P("gx", "gy"),
        P("gx", "gy", None),
        P("gx"),
        P(),
        P(),
        P(),
        P("gy"),
        P(),
        P(),
    )
    return jax.shard_map(
        body,
        mesh=mesh,
        in_specs=placed,
        out_specs=(P(None, "gx", "gy", None), P(None, "gx", "gy", None), P("gx", "gy")),
        check_vma=False,
    )
```

profile of v0, /device:TPU:0, one launch (start us, length us, event | category | flops | bytes accessed | tf_op | source)
XLA Modules:
  0.0 497.4 jit_solution(11973510932062096920)
XLA Ops:
  16.5 3.5 collective-permute-start.2
  23.5 4.4 collective-permute-done.3
  27.9 4.2 select_maximum_fusion.4
  33.9 2.8 fusion.48
  37.4 2.9 convert_reduce_fusion.1
  44.3 4.8 fusion.58
  49.1 38.3 %all-gather.5.cloned.1.call-done = f32[16,64,512]{2,1,0:T(8,128)} async-done(((f32[16,16,512]{2,1,0:T(8,128)}), f32[16,64,512]{2,1,0:T(8,128)}) %all-gather.5.cloned.1.call-update) | async-done | bytes 2097168 | tf_op jit(solution)/shard_map/all_gather | solution.py:143
  87.4 2.9 copy.70
  92.9 11.9 %all-gather = f32[4,4,16]{2,1,0:T(4,128)S(1)} all-gather(f32[1,4,16]{2,1,0:T(4,128)S(1)} %bitcast.214), channel_id=1, replica_groups=mesh['gx'=8,'gy'=4] {'gy'}, dimensions={0}, use_global_device_ids=true | all-gather | bytes 1280 | tf_op jit(solution)/shard_map/all_gather | solution.py:154
  106.0 8.8 %copy.50 = f32[3,16,16,512]{2,1,0,3:T(8,128)} copy(f32[3,16,16,512]{3,2,1,0:T(8,128)S(1)} %pad_maximum_fusion) | data formatting | bytes 3145728 | tf_op jit(solution)/shard_map/stack | solution.py:162
  114.8 8.9 %reshape.89 = f32[8,1,49152]{2,1,0:T(1,128)S(1)} reshape(f32[512,3,16,16]{3,2,1,0:T(8,128)} %bitcast.186) | data formatting | bytes 3145728
  123.7 24.6 %all_to_all.66 = f32[8,1,49152]{2,1,0:T(1,128)S(1)} all-to-all(f32[8,1,49152]{2,1,0:T(1,128)S(1)} %reshape.89), channel_id=1, replica_groups=mesh['gx'=8,'gy'=4] {'gx'}, dimensions={0} | all-to-all | bytes 3145728 | tf_op jit(solution)/shard_map/all_to_all | solution.py:108
  148.8 4.4 reduce
  153.2 8.7 %reshape.90 = f32[512,3,16,16]{3,2,1,0:T(8,128)} reshape(f32[8,49152]{1,0:T(8,128)S(1)} %reduce) | data formatting | bytes 3145728
  162.0 8.1 %copy.51 = f32[3,16,16,8,64]{4,2,1,3,0:T(8,128)S(1)} copy(f32[3,16,16,8,64]{2,1,0,4,3:T(8,128)} %bitcast.188) | data formatting | bytes 3145728 | tf_op jit(solution)/shard_map/all_to_all | solution.py:108
  171.9 5.2 %fusion.65 = f32[3,1024,128]{2,1,0:T(8,128)} fusion(f32[3,128,1024]{2,1,0:T(8,128)} %reshape.79, f32[128,128]{1,0:T(8,128)S(1)} %copy-done), kind=kOutput, calls=%fused_computation.160 | convolution fusion | flops 603979776 | bytes 3211264 | tf_op jit(solution)/shard_map/zk,fkm->fzm/dot_general | solution.py:111
  179.5 3.0 reshape.91
  182.5 24.5 %all_to_all.67 = f32[8,1,49152]{2,1,0:T(1,128)S(1)} all-to-all(f32[8,1,49152]{2,1,0:T(1,128)} %reshape.91), channel_id=1, replica_groups=mesh['gx'=8,'gy'=4] {'gx'}, dimensions={0} | all-to-all | bytes 3145728 | tf_op jit(solution)/shard_map/all_to_all | solution.py:114
  207.0 6.2 %reduce.1 = f32[8,49152]{1,0:T(8,128)} reduce(f32[8,1,49152]{2,1,0:T(1,128)S(1)} %all_to_all.67, f32[]{:T(128)} %broadcast.158), dimensions={1}, to_apply=%all_to_all.51.reduce_sub_computation | reduce | bytes 3145732 | tf_op jit(solution)/shard_map/all_to_all | solution.py:114
  213.2 2.7 reshape.92
  215.8 3.5 copy.56
  219.3 3.8 all_to_all.54
  233.3 4.4 collective-permute-done.7
  251.2 4.0 collective-permute-start.8
  260.3 4.6 collective-permute-start.10
  273.0 5.7 %select_maximum_fusion = f32[6,18,18,514]{3,2,1,0:T(8,128)S(1)} fusion(f32[6,18,1,512]{3,2,1,0:T(1,128)} %collective-permute-done.11, f32[6,18,1,512]{3,2,1,0:T(1,128)} %collective-permute-done.10, f32[6,1,16,512]{3,2,1,0:T(8,128)} %copy-done.25, f32[6,16,16,512]{3,2,1,0:T(8,128)S(1)} %copy-done.2, f32[6,1,16,512]{3,2,1,0:T(8,128)S(1)} %collective-permute-done.8), kind=kLoop, calls=%fused_computation.9 | loop fusion | flops 11990592 | bytes 7978176 | tf_op jit(solution)/shard_map/concatenate | solution.py:21
  282.4 2.8 copy.55
  287.6 2.9 copy.57
  293.8 5.7 %fusion.35 = (f32[1,16,16,512]{3,2,1,0:T(8,128)S(1)}, f32[1,16,16,512]{3,2,1,0:T(8,128)}) fusion(f32[16,16,512]{2,1,0:T(8,128)} %squeeze.117, f32[18,18,514]{2,1,0:T(8,128)S(1)} %get-tuple-element.21, f32[18,18,514]{2,1,0:T(8,128)} %get-tuple-element.22, f32[18,18,514]{2,1,0:T(8,128)} %get-tuple-element.18, f32[16,16,512]{2,1,0:T(8,128)S(1)} %copy-done.5, ...), kind=kLoop, calls=%fused_computation.92 | loop fusion | flops 1966080 | bytes 8388608 | tf_op jit(solution)/shard_map/stack | solution.py:61
  299.5 32.2 %all-gather.7.cloned.1.call-done = f32[16,64,512]{2,1,0:T(8,128)} async-done(((f32[16,16,512]{2,1,0:T(8,128)}), f32[16,64,512]{2,1,0:T(8,128)}) %all-gather.7.cloned.1.call-update) | async-done | bytes 2097168 | tf_op jit(solution)/shard_map/all_gather | solution.py:143
  331.7 2.9 copy.73
  334.6 3.2 multiply_subtract_fusion
  337.9 11.9 %all-gather.1 = f32[4,4,16]{2,1,0:T(4,128)S(1)} all-gather(f32[1,4,16]{2,1,0:T(4,128)S(1)} %bitcast.215), channel_id=1, replica_groups=mesh['gx'=8,'gy'=4] {'gy'}, dimensions={0}, use_global_device_ids=true | all-gather | bytes 1280 | tf_op jit(solution)/shard_map/all_gather | solution.py:154
  350.9 8.8 %copy.59 = f32[3,16,16,512]{2,1,0,3:T(8,128)} copy(f32[3,16,16,512]{3,2,1,0:T(8,128)S(1)} %pad_maximum_fusion.1) | data formatting | bytes 3145728 | tf_op jit(solution)/shard_map/stack | solution.py:162
  359.7 8.9 %reshape.93 = f32[8,1,49152]{2,1,0:T(1,128)S(1)} reshape(f32[512,3,16,16]{3,2,1,0:T(8,128)} %bitcast.187) | data formatting | bytes 3145728
  368.6 24.6 %all_to_all.68 = f32[8,1,49152]{2,1,0:T(1,128)S(1)} all-to-all(f32[8,1,49152]{2,1,0:T(1,128)S(1)} %reshape.93), channel_id=1, replica_groups=mesh['gx'=8,'gy'=4] {'gx'}, dimensions={0} | all-to-all | bytes 3145728 | tf_op jit(solution)/shard_map/all_to_all | solution.py:108
  393.2 4.4 reduce.2
  397.6 8.7 %reshape.94 = f32[512,3,16,16]{3,2,1,0:T(8,128)} reshape(f32[8,49152]{1,0:T(8,128)S(1)} %reduce.2) | data formatting | bytes 3145728
  406.3 8.1 %copy.60 = f32[3,16,16,8,64]{4,2,1,3,0:T(8,128)S(1)} copy(f32[3,16,16,8,64]{2,1,0,4,3:T(8,128)} %bitcast.189) | data formatting | bytes 3145728 | tf_op jit(solution)/shard_map/all_to_all | solution.py:108
  416.2 5.2 %fusion.63 = f32[3,1024,128]{2,1,0:T(8,128)} fusion(f32[3,128,1024]{2,1,0:T(8,128)} %reshape.82, f32[128,128]{1,0:T(8,128)S(1)} %copy-done), kind=kOutput, calls=%fused_computation.158 | convolution fusion | flops 603979776 | bytes 3211264 | tf_op jit(solution)/shard_map/zk,fkm->fzm/dot_general | solution.py:111
  421.4 2.7 copy.62
  424.1 3.0 reshape.95
  427.1 24.5 %all_to_all.69 = f32[8,1,49152]{2,1,0:T(1,128)S(1)} all-to-all(f32[8,1,49152]{2,1,0:T(1,128)} %reshape.95), channel_id=1, replica_groups=mesh['gx'=8,'gy'=4] {'gx'}, dimensions={0} | all-to-all | bytes 3145728 | tf_op jit(solution)/shard_map/all_to_all | solution.py:114
  451.6 6.2 %reduce.3 = f32[8,49152]{1,0:T(8,128)} reduce(f32[8,1,49152]{2,1,0:T(1,128)S(1)} %all_to_all.69, f32[]{:T(128)} %broadcast.158), dimensions={1}, to_apply=%all_to_all.58.reduce_sub_computation | reduce | bytes 3145732 | tf_op jit(solution)/shard_map/all_to_all | solution.py:114
  457.7 2.7 reshape.96
  460.4 3.5 copy.64
  463.9 2.8 all_to_all.61
  475.9 4.4 collective-permute-done.15
  (158 shorter events, 95.8 us)
Async XLA Ops:
  7.2 164.7 %copy-start = (f32[128,128]{1,0:T(8,128)S(1)}, f32[128,128]{1,0:T(8,128)}, u32[]{:S(2)}) copy-start(f32[128,128]{1,0:T(8,128)} %param.21) | copy-start | bytes 196612
  7.2 80.2 %all-gather.5.cloned.1.call-start = ((), (), s32[]{:S(2)}) async-start(), calls=%async_computation.4 | async-start | bytes 2621440 | tf_op jit(solution)/shard_map/all_gather | solution.py:143
  8.3 3.7 collective-permute-start
  10.7 5.4 %collective-permute-start.1 = (f32[6,1,16,512]{3,2,1,0:T(8,128)S(1)}, f32[6,1,16,512]{3,2,1,0:T(8,128)S(1)}, u32[]{:S(2)}, u32[]{:S(2)}) collective-permute-start(f32[6,1,16,512]{3,2,1,0:T(8,128)S(1)} %get-tuple-element.47), channel_id=1, source_target_pairs={{4,0},{8,4},{12,8},{16,12},{20,16},{24,20},{28,24},{5,1},{9,5},{13... | collective-permute-start | bytes 589832 | tf_op jit(solution)/shard_map/ppermute | solution.py:25
  16.5 6.9 %collective-permute-start.2 = (f32[6,18,1,512]{3,2,1,0:T(1,128)S(1)}, f32[6,18,1,512]{3,2,1,0:T(1,128)S(1)}, u32[]{:S(2)}, u32[]{:S(2)}) collective-permute-start(f32[6,18,1,512]{3,2,1,0:T(1,128)S(1)} %get-tuple-element.32), channel_id=1, source_target_pairs={{0,1},{1,2},{2,3},{4,5},{5,6},{6,7},{8,9},{9,10},{10,11},{12,13},{... | collective-permute-start | bytes 663560 | tf_op jit(solution)/shard_map/ppermute | solution.py:23
  20.1 7.8 %collective-permute-start.3 = (f32[6,18,1,512]{3,2,1,0:T(1,128)S(1)}, f32[6,18,1,512]{3,2,1,0:T(1,128)S(1)}, u32[]{:S(2)}, u32[]{:S(2)}) collective-permute-start(f32[6,18,1,512]{3,2,1,0:T(1,128)S(1)} %get-tuple-element.33), channel_id=1, source_target_pairs={{1,0},{2,1},{3,2},{5,4},{6,5},{7,6},{9,8},{10,9},{11,10},{13,12},{... | collective-permute-start | bytes 663560 | tf_op jit(solution)/shard_map/ppermute | solution.py:25
  32.1 1.8 copy-start.4
  33.9 3.4 copy-start.27
  36.7 295.0 %all-gather.7.cloned.1.call-start = ((), (), s32[]{:S(2)}) async-start(), calls=%async_computation.5 | async-start | bytes 2621440 | tf_op jit(solution)/shard_map/all_gather | solution.py:143
  37.3 7.0 %copy-start.7 = (f32[18,18,514]{2,1,0:T(8,128)S(1)}, f32[18,18,514]{2,1,0:T(8,128)}, u32[]{:S(2)}) copy-start(f32[18,18,514]{2,1,0:T(8,128)} %get-tuple-element.28) | copy-start | bytes 1998436
  42.0 62.8 %copy-start.8 = (f32[8192,16]{0,1:T(8,128)}, f32[8192,16]{0,1:T(8,128)S(1)}, u32[]{:S(2)}) copy-start(f32[8192,16]{0,1:T(8,128)S(1)} %convert_reduce_fusion) | copy-start | bytes 1572868
  87.4 2.9 copy-start.11
  87.4 2.9 copy-start.28
  87.4 2.9 copy-start.29
  90.3 14.5 %copy-start.15 = (f32[2,8,16,512]{3,1,2,0:T(8,128)S(1)}, f32[2,8,16,512]{3,1,2,0:T(8,128)}, u32[]{:S(2)}) copy-start(f32[2,8,16,512]{3,1,2,0:T(8,128)} %copy.69) | copy-start | bytes 1572868
  90.3 15.5 %copy-start.17 = (f32[1,16,16,512]{3,2,1,0:T(8,128)S(1)}, f32[1,16,16,512]{3,2,1,0:T(8,128)}, u32[]{:S(2)}) copy-start(f32[1,16,16,512]{3,2,1,0:T(8,128)} %get-tuple-element.40) | copy-start | bytes 1572868
  90.3 15.5 %copy-start.18 = (f32[1,16,16,512]{3,2,1,0:T(8,128)S(1)}, f32[1,16,16,512]{3,2,1,0:T(8,128)}, u32[]{:S(2)}) copy-start(f32[1,16,16,512]{3,2,1,0:T(8,128)} %get-tuple-element.41) | copy-start | bytes 1572868
  219.3 6.1 %copy-start.30 = (f32[8]{0:T(128)S(1)}, f32[8]{0:T(128)}, u32[]{:S(2)}) copy-start(f32[8]{0:T(128)} %param.18) | copy-start | bytes 100
  219.3 6.1 %copy-start.31 = (s32[16]{0:T(128)S(1)}, s32[16]{0:T(128)}, u32[]{:S(2)}) copy-start(s32[16]{0:T(128)} %param.15) | copy-start | bytes 196
  219.3 6.1 %copy-start.32 = (f32[8]{0:T(128)S(1)}, f32[8]{0:T(128)}, u32[]{:S(2)}) copy-start(f32[8]{0:T(128)} %param.17) | copy-start | bytes 100
  219.3 6.1 %copy-start.33 = (f32[8]{0:T(128)S(1)}, f32[8]{0:T(128)}, u32[]{:S(2)}) copy-start(f32[8]{0:T(128)} %param.16) | copy-start | bytes 100
  224.1 2.7 collective-permute-start.4
  225.5 4.0 collective-permute-start.5
  229.7 3.6 collective-permute-start.6
  231.0 6.7 %collective-permute-start.7 = (f32[3,18,1,512]{3,2,1,0:T(1,128)S(1)}, f32[3,18,1,512]{3,2,1,0:T(1,128)S(1)}, u32[]{:S(2)}, u32[]{:S(2)}) collective-permute-start(f32[3,18,1,512]{3,2,1,0:T(1,128)S(1)} %get-tuple-element.52), channel_id=1, source_target_pairs={{1,0},{2,1},{3,2},{5,4},{6,5},{7,6},{9,8},{10,9},{11,10},{13,12},{... | collective-permute-start | bytes 331784 | tf_op jit(solution)/shard_map/ppermute | solution.py:25
  239.5 1.9 copy-start.3
  251.1 7.9 %copy-start.1 = (f32[6,16,16,512]{3,2,1,0:T(8,128)}, f32[6,16,16,512]{3,2,1,0:T(8,128)S(1)}, u32[]{:S(2)}) copy-start(f32[6,16,16,512]{3,2,1,0:T(8,128)S(1)} %get-tuple-element.6) | copy-start | bytes 9437188
  251.2 5.6 %collective-permute-start.8 = (f32[6,1,16,512]{3,2,1,0:T(8,128)S(1)}, f32[6,1,16,512]{3,2,1,0:T(8,128)S(1)}, u32[]{:S(2)}, u32[]{:S(2)}) collective-permute-start(f32[6,1,16,512]{3,2,1,0:T(8,128)S(1)} %get-tuple-element.45), channel_id=1, source_target_pairs={{0,4},{4,8},{8,12},{12,16},{16,20},{20,24},{24,28},{1,5},{5,9},{9,... | collective-permute-start | bytes 589832 | tf_op jit(solution)/shard_map/ppermute | solution.py:23
  255.2 3.9 collective-permute-start.9
  259.1 7.3 %copy-start.25 = (f32[6,1,16,512]{3,2,1,0:T(8,128)}, f32[6,1,16,512]{3,2,1,0:T(8,128)S(1)}, u32[]{:S(2)}) copy-start(f32[6,1,16,512]{3,2,1,0:T(8,128)S(1)} %collective-permute-done.9) | copy-start | bytes 589828
  260.3 11.6 %collective-permute-start.10 = (f32[6,18,1,512]{3,2,1,0:T(1,128)}, f32[6,18,1,512]{3,2,1,0:T(1,128)}, u32[]{:S(2)}, u32[]{:S(2)}) collective-permute-start(f32[6,18,1,512]{3,2,1,0:T(1,128)} %get-tuple-element.30), channel_id=1, source_target_pairs={{0,1},{1,2},{2,3},{4,5},{5,6},{6,7},{8,9},{9,10},{10,11},{12,13},{... | collective-permute-start | bytes 663560 | tf_op jit(solution)/shard_map/ppermute | solution.py:23
  264.9 8.1 %collective-permute-start.11 = (f32[6,18,1,512]{3,2,1,0:T(1,128)}, f32[6,18,1,512]{3,2,1,0:T(1,128)}, u32[]{:S(2)}, u32[]{:S(2)}) collective-permute-start(f32[6,18,1,512]{3,2,1,0:T(1,128)} %get-tuple-element.31), channel_id=1, source_target_pairs={{1,0},{2,1},{3,2},{5,4},{6,5},{7,6},{9,8},{10,9},{11,10},{13,12},{... | collective-permute-start | bytes 663560 | tf_op jit(solution)/shard_map/ppermute | solution.py:25
  268.0 5.0 %copy-start.2 = (f32[6,16,16,512]{3,2,1,0:T(8,128)S(1)}, f32[6,16,16,512]{3,2,1,0:T(8,128)}, u32[]{:S(2)}) copy-start(f32[6,16,16,512]{3,2,1,0:T(8,128)} %copy-done.1) | copy-start | bytes 9437188
  278.8 1.8 copy-start.5
  278.8 1.8 copy-start.13
  287.5 5.2 %copy-start.10 = (f32[16,16,512]{2,1,0:T(8,128)S(1)}, f32[16,16,512]{2,1,0:T(8,128)}, u32[]{:S(2)}) copy-start(f32[16,16,512]{2,1,0:T(8,128)} %fusion.25) | copy-start | bytes 1572868
  331.7 2.9 copy-start.12
  334.6 15.2 %copy-start.9 = (f32[8192,16]{0,1:T(8,128)S(1)}, f32[8192,16]{0,1:T(8,128)}, u32[]{:S(2)}) copy-start(f32[8192,16]{0,1:T(8,128)} %copy-done.8) | copy-start | bytes 1572868
  334.6 15.2 %copy-start.14 = (f32[2,8,16,512]{3,1,2,0:T(8,128)S(1)}, f32[2,8,16,512]{3,1,2,0:T(8,128)}, u32[]{:S(2)}) copy-start(f32[2,8,16,512]{3,1,2,0:T(8,128)} %copy.72) | copy-start | bytes 1572868
  334.6 16.1 %copy-start.16 = (f32[1,16,16,512]{3,2,1,0:T(8,128)S(1)}, f32[1,16,16,512]{3,2,1,0:T(8,128)}, u32[]{:S(2)}) copy-start(f32[1,16,16,512]{3,2,1,0:T(8,128)} %get-tuple-element.54) | copy-start | bytes 1572868
  466.7 5.5 %copy-start.6 = (f32[3,16,16,512]{3,2,1,0:T(8,128)}, f32[3,16,16,512]{3,2,1,0:T(8,128)S(1)}, u32[]{:S(2)}) copy-start(f32[3,16,16,512]{3,2,1,0:T(8,128)S(1)} %all_to_all.61) | copy-start | bytes 4718596
  466.8 2.6 collective-permute-start.12
  468.1 4.0 collective-permute-start.13
  472.3 3.6 collective-permute-start.14
  473.6 6.7 %collective-permute-start.15 = (f32[3,18,1,512]{3,2,1,0:T(1,128)S(1)}, f32[3,18,1,512]{3,2,1,0:T(1,128)S(1)}, u32[]{:S(2)}, u32[]{:S(2)}) collective-permute-start(f32[3,18,1,512]{3,2,1,0:T(1,128)S(1)} %get-tuple-element.50), channel_id=1, source_target_pairs={{1,0},{2,1},{3,2},{5,4},{6,5},{7,6},{9,8},{10,9},{11,10},{13,12},{... | collective-permute-start | bytes 331784 | tf_op jit(solution)/shard_map/ppermute | solution.py:25
  486.3 1.0 copy-start.22
  486.9 1.1 copy-start.19
  488.7 1.7 copy-start.26
  (4 other events, 4.2 us)
Sparse Core Ops, SparseCore 0:
  36.9 50.5 all-gather.4
  282.6 49.1 all-gather.6
where the time goes:
time: 505 us; the launch traced here: 497 us
  local copies, waits for them, and re-layouts  145 us (29%)
  blocking collectives  122 us (24%)
  waiting for transfers between devices  96.1 us (19%)
  other arithmetic  70.7 us (14%)
  starting transfers between devices  31.3 us (6%)
  matrix products  17.4 us (3%)
  between operations  15 us (3%)
    all_gather x2, waiting for transfers between devices, body(): piece = lax.all_gather(velocity[2], 'gy', axis=1, tiled=True)  70.5 us
    unnamed x88, local copies, waits for them, and re-layouts  65.1 us
    all_to_all x2, blocking collectives, damp_columns(): lax.all_to_all(velocity, 'gx', split_axis=3, concat_axis=1, tiled=True)  49.2 us
    all_to_all x2, blocking collectives, damp_columns(): return lax.all_to_all(damped, 'gx', split_axis=1, concat_axis=3, tiled=True)  48.9 us
    all_gather x2, blocking collectives, body(): all_force = lax.all_gather(force, 'gy', axis=1, tiled=True)  23.8 us
    ppermute x8, waiting for transfers between devices, extended(): lax.ppermute(head, axis, [((i + 1) % count, i) for i in range(ends)])  22 us
    ppermute x8, starting transfers between devices, extended(): lax.ppermute(tail, axis, [(i, (i + 1) % count) for i in range(ends)])  19.7 us
    another operation x2, local copies, waits for them, and re-layouts, body(): jnp.stack([velocity[0], velocity[1], vertical.reshape(depth_cells, side_c...  17.6 us
  transfers between devices with their start and end apart: 18, of which 13 were waited for; matrix products, arithmetic and copies ran while one was open for 8% of the time, Pallas kernels for 0%

commit v1 on v0

--- a/solution.py
+++ b/solution.py
@@ -1,6 +1,9 @@
+import functools
 import jax
 import jax.numpy as jnp
 from jax import lax
+from jax.experimental import pallas as pl
+from jax.experimental.pallas import tpu as pltpu
 from jax.sharding import PartitionSpec as P
 
 STEPS = 2
@@ -168,6 +171,482 @@
     return (velocity, stress, pier_velocity)
 
 
+SIDE = 4
+LANES = 128
+ROWS = 8
+MESH = pl.DeviceIdType.MESH
+Z_GHOSTS = ((2, -1), (4, 1), (5, 1))
+Y_GHOSTS = ((1, -1), (3, 1), (5, 1))
+
+
+def shift_x(a, ahead):
+    lane = lax.broadcasted_iota(jnp.int32, a.shape, 1)
+    width = a.shape[1]
+    if ahead:
+        return jnp.where(lane == width - 1, 0.0, pltpu.roll(a, width - 1, 1))
+    return jnp.where(lane == 0, 0.0, pltpu.roll(a, 1, 1))
+
+
+def fused(
+    n, ng, v_hbm, s_hbm, b_hbm, coef_hbm, w_ref, imp_ref, row_ref, col_ref, damp_ref,
+    v_out, s_out, w_out,
+    v_ext, s_ext, buoy, coef, acc, pin, pout, um, wbuf, sg_send, sg_recv, yg_send, yg_recv,
+    load_sem, zs_send, zs_recv, cf_send, cf_recv, ys_send, ys_recv,
+    f_send, f_recv, r_send, r_recv, u_send, u_recv, y_send, y_recv, o_sem,
+):
+    me = lax.axis_index("gx")
+    g = lax.axis_index("gy")
+    depth, side, line = buoy.shape
+    tiles = line // LANES
+    inner = pl.ds(ROWS, side)
+
+    def piece(j):
+        return (
+            pl.ds(pl.multiple_of((j // tiles) * ROWS, ROWS), ROWS),
+            pl.ds(pl.multiple_of((j % tiles) * LANES, LANES), LANES),
+        )
+
+    loads = {}
+    for slot, f in enumerate((1, 3, 5, 2, 4, 0)):
+        loads[("s", f)] = pltpu.make_async_copy(
+            s_hbm.at[f], s_ext.at[f, pl.ds(1, depth), inner, :], load_sem.at[slot]
+        )
+    loads["b"] = pltpu.make_async_copy(b_hbm, buoy, load_sem.at[6])
+    for f in range(3):
+        loads[("v", f)] = pltpu.make_async_copy(
+            v_hbm.at[f], v_ext.at[f, pl.ds(1, depth), inner, :], load_sem.at[7 + f]
+        )
+    loads["c"] = pltpu.make_async_copy(coef_hbm, coef.at[:, pl.ds(1, depth)], load_sem.at[10])
+    for copy in loads.values():
+        copy.start()
+
+    plane = jnp.zeros((side, line), jnp.float32)
+    for f, way in Z_GHOSTS:
+        s_ext[f, 0 if way < 0 else depth + 1, inner, :] = plane
+    edge = jnp.zeros((ROWS, line), jnp.float32)
+
+    def clear(k, carry):
+        for f, way in Y_GHOSTS:
+            s_ext[f, k, pl.ds(0 if way < 0 else ROWS + side, ROWS), :] = edge
+        for f in range(3):
+            v_ext[f, k, pl.ds(0, ROWS), :] = edge
+            v_ext[f, k, pl.ds(ROWS + side, ROWS), :] = edge
+        return carry
+
+    lax.fori_loop(0, depth + 2, clear, 0)
+    for c in range(3):
+        coef[c, 0] = jnp.zeros((ROWS, LANES), jnp.float32)
+        coef[c, depth + 1] = jnp.zeros((ROWS, LANES), jnp.float32)
+        pout[c, 0] = jnp.zeros((ROWS, LANES), jnp.float32)
+        pout[c, n * depth + 1] = jnp.zeros((ROWS, LANES), jnp.float32)
+
+    barrier = pltpu.get_barrier_semaphore()
+    for d in range(1, n):
+        pl.semaphore_signal(
+            barrier, inc=1, device_id=(lax.rem(me + d, n), g), device_id_type=MESH
+        )
+    for d in range(1, ng):
+        pl.semaphore_signal(
+            barrier, inc=1, device_id=(me, lax.rem(g + d, ng)), device_id_type=MESH
+        )
+    pl.semaphore_wait(barrier, n - 1 + ng - 1)
+
+    def z_copy(i):
+        f, way = Z_GHOSTS[i]
+        return pltpu.make_async_remote_copy(
+            src_ref=s_hbm.at[f, depth - 1 if way < 0 else 0],
+            dst_ref=s_ext.at[f, 0 if way < 0 else depth + 1, inner, :],
+            send_sem=zs_send.at[i],
+            recv_sem=zs_recv.at[i],
+            device_id=(me - way, g),
+            device_id_type=MESH,
+        )
+
+    def c_copy(way):
+        i = (way + 1) // 2
+        return pltpu.make_async_remote_copy(
+            src_ref=coef_hbm.at[:, depth - 1 if way < 0 else 0],
+            dst_ref=coef.at[:, 0 if way < 0 else depth + 1],
+            send_sem=cf_send.at[i],
+            recv_sem=cf_recv.at[i],
+            device_id=(me - way, g),
+            device_id_type=MESH,
+        )
+
+    def y_stress(i):
+        f, way = Y_GHOSTS[i]
+        return pltpu.make_async_remote_copy(
+            src_ref=sg_send.at[i],
+            dst_ref=sg_recv.at[i],
+            send_sem=ys_send.at[i],
+            recv_sem=ys_recv.at[i],
+            device_id=(me, g - way),
+            device_id_type=MESH,
+        )
+
+    not_ends = {
+        -1: (me > 0, me < n - 1, g > 0, g < ng - 1),
+        1: (me < n - 1, me > 0, g < ng - 1, g > 0),
+    }
+
+    for i, (f, way) in enumerate(Z_GHOSTS):
+        @pl.when(not_ends[way][1])
+        def _(i=i):
+            z_copy(i).start()
+    for way in (-1, 1):
+        @pl.when(not_ends[way][1])
+        def _(way=way):
+            c_copy(way).start()
+    for i, (f, way) in enumerate(Y_GHOSTS):
+        loads[("s", f)].wait()
+        sg_send[i] = s_ext[f, pl.ds(1, depth), ROWS + side - 1 if way < 0 else ROWS, :]
+
+        @pl.when(not_ends[way][3])
+        def _(i=i):
+            y_stress(i).start()
+    for key, copy in loads.items():
+        if key not in (("s", 1), ("s", 3), ("s", 5)):
+            copy.wait()
+
+    ids = lax.broadcasted_iota(jnp.int32, (side, LANES), 0) + g * side
+    first = row_ref[0:1, :]
+    in_rows = jnp.where((ids >= first) & (ids < first + SIDE), 1.0, 0.0)
+    across = lax.broadcasted_iota(jnp.int32, (LANES, line), 1)
+    start = jnp.concatenate([col_ref[...]] * tiles, axis=1)
+    in_cols = jnp.where((across >= start) & (across < start + SIDE), 1.0, 0.0)
+
+    for i, (f, way) in enumerate(Z_GHOSTS):
+        @pl.when(not_ends[way][0])
+        def _(i=i):
+            z_copy(i).wait_recv()
+
+        @pl.when(not_ends[way][1])
+        def _(i=i):
+            z_copy(i).wait_send()
+    for way in (-1, 1):
+        @pl.when(not_ends[way][0])
+        def _(way=way):
+            c_copy(way).wait_recv()
+
+        @pl.when(not_ends[way][1])
+        def _(way=way):
+            c_copy(way).wait_send()
+    for i, (f, way) in enumerate(Y_GHOSTS):
+        @pl.when(not_ends[way][2])
+        def _(i=i, f=f, way=way):
+            y_stress(i).wait_recv()
+            s_ext[f, pl.ds(1, depth), ROWS - 1 if way < 0 else ROWS + side, :] = sg_recv[i]
+
+        @pl.when(not_ends[way][3])
+        def _(i=i):
+            y_stress(i).wait_send()
+
+    def cells(ref, f, k, shift=0, begin=ROWS, rows=None):
+        return ref[f, k, pl.ds(begin + shift, side if rows is None else rows), :]
+
+    def speed_x(i, carry):
+        k = i + 1
+        xx, xy, xz = cells(s_ext, 0, k), cells(s_ext, 3, k), cells(s_ext, 4, k)
+        total = (xx - shift_x(xx, False)) + (cells(s_ext, 3, k, 1) - xy)
+        total = total + (cells(s_ext, 4, k + 1) - xz)
+        acc[0, i] = cells(v_ext, 0, k) + (grid_ratio * buoy[i]) * total
+        return carry
+
+    def speed_y(i, carry):
+        k = i + 1
+        xy, yy, yz = cells(s_ext, 3, k), cells(s_ext, 1, k), cells(s_ext, 5, k)
+        total = (shift_x(xy, True) - xy) + (yy - cells(s_ext, 1, k, -1))
+        total = total + (cells(s_ext, 5, k + 1) - yz)
+        acc[1, i] = cells(v_ext, 1, k) + (grid_ratio * buoy[i]) * total
+        return carry
+
+    def speed_z(i, carry):
+        k = i + 1
+        xz, yz, zz = cells(s_ext, 4, k), cells(s_ext, 5, k), cells(s_ext, 2, k)
+        total = (shift_x(xz, True) - xz) + (cells(s_ext, 5, k, 1) - yz)
+        total = total + (zz - cells(s_ext, 2, k - 1))
+        acc[2, i] = cells(v_ext, 2, k) + (grid_ratio * buoy[i]) * total
+        return carry
+
+    def wide(c, k, rows):
+        tile = jnp.concatenate([coef[c, k]] * tiles, axis=1)
+        return jnp.concatenate([tile] * (rows // ROWS), axis=0)
+
+    def normals(k, begin, rows):
+        at = functools.partial(cells, begin=begin, rows=rows)
+        lame, shear, relax = (wide(c, k, rows) for c in range(3))
+        vx, vy, vz = at(v_ext, 0, k), at(v_ext, 1, k), at(v_ext, 2, k)
+        ex = shift_x(vx, True) - vx
+        ey = at(v_ext, 1, k, 1) - vy
+        ez = at(v_ext, 2, k + 1) - vz
+        modulus = lame + 2.0 * shear
+        for f, own, others in ((0, ex, ey + ez), (1, ey, ex + ez), (2, ez, ex + ey)):
+            s_ext[f, k, pl.ds(begin, rows), :] = relax * at(s_ext, f, k) + grid_ratio * (
+                modulus * own + lame * others
+            )
+
+    def shears(k, begin, rows):
+        at = functools.partial(cells, begin=begin, rows=rows)
+        shear, relax = wide(1, k, rows), wide(2, k, rows)
+        shear = grid_ratio * shear
+        vx, vy, vz = at(v_ext, 0, k), at(v_ext, 1, k), at(v_ext, 2, k)
+        xy = (vx - at(v_ext, 0, k, -1)) + (vy - shift_x(vy, False))
+        xz = (vx - at(v_ext, 0, k - 1)) + (vz - shift_x(vz, False))
+        yz = (vy - at(v_ext, 1, k - 1)) + (vz - at(v_ext, 2, k, -1))
+        for f, strain in ((3, xy), (4, xz), (5, yz)):
+            s_ext[f, k, pl.ds(begin, rows), :] = relax * at(s_ext, f, k) + shear * strain
+
+    def there(step, f, d):
+        t = lax.rem(me + d, n)
+        ys, xs = piece(t)
+        src = acc.at[f, :, ys, xs]
+        dst = pin.at[f, pl.ds(me * depth, depth)]
+        if d == 0:
+            return pltpu.make_async_copy(src, dst, f_recv.at[step, f, 0])
+        return pltpu.make_async_remote_copy(
+            src_ref=src, dst_ref=dst, send_sem=f_send.at[step, f, d],
+            recv_sem=f_recv.at[step, f, d], device_id=(t, g), device_id_type=MESH,
+        )
+
+    def back(step, f, d):
+        t = lax.rem(me + d, n)
+        ys, xs = pl.ds(pl.multiple_of((me // tiles) * ROWS + ROWS, ROWS), ROWS), piece(me)[1]
+        src = pout.at[f, pl.ds(t * depth, depth + 2)]
+        dst = v_ext.at[f, :, ys, xs]
+        if d == 0:
+            return pltpu.make_async_copy(src, dst, r_recv.at[step, f, 0])
+        return pltpu.make_async_remote_copy(
+            src_ref=src, dst_ref=dst, send_sem=r_send.at[step, f, d],
+            recv_sem=r_recv.at[step, f, d], device_id=(t, g), device_id_type=MESH,
+        )
+
+    def start_all(make, step, f):
+        for d in list(range(1, n)) + [0]:
+            make(step, f, d).start()
+
+    def wait_sent(make, step, f):
+        for d in range(1, n):
+            make(step, f, d).wait_send()
+
+    def wait_got(make, step, f):
+        make(step, f, 0).wait()
+        for d in range(1, n):
+            make(step, f, d).wait_recv()
+
+    def share(step, d):
+        return pltpu.make_async_remote_copy(
+            src_ref=um.at[step, 0], dst_ref=um.at[step, d],
+            send_sem=u_send.at[step, d], recv_sem=u_recv.at[step, d],
+            device_id=(me, lax.rem(g + d, ng)), device_id_type=MESH,
+        )
+
+    def y_speed(step, f, i):
+        return pltpu.make_async_remote_copy(
+            src_ref=yg_send.at[step, f, i], dst_ref=yg_recv.at[step, f, i],
+            send_sem=y_send.at[step, f, i], recv_sem=y_recv.at[step, f, i],
+            device_id=(me, g + 1 - 2 * i), device_id_type=MESH,
+        )
+
+    has_next, has_last = g < ng - 1, g > 0
+    planes = pl.ds(0, depth + 2)
+
+    for step in range(STEPS):
+        if step > 0:
+            for f in range(3):
+                wait_sent(there, step - 1, f)
+        lax.fori_loop(0, depth, speed_z, 0)
+        flat = acc[2].reshape(depth * side, line)
+        part = lax.dot_general(
+            flat, in_cols, (((1,), (1,)), ((), ())),
+            precision=lax.Precision.HIGHEST, preferred_element_type=jnp.float32,
+        ).reshape(depth, side, LANES)
+        um[step, 0, pl.ds(0, depth), :] = jnp.sum(part * in_rows[None], axis=1)
+        um[step, 0, pl.ds(depth, depth), :] = w_ref[...]
+        um[step, 0, pl.ds(2 * depth, ROWS), :] = imp_ref[...]
+        for d in range(1, ng):
+            share(step, d).start()
+        lax.fori_loop(0, depth, speed_x, 0)
+        start_all(there, step, 0)
+        lax.fori_loop(0, depth, speed_y, 0)
+        start_all(there, step, 1)
+        for d in range(1, ng):
+            share(step, d).wait()
+        every = um[step, 0]
+        for d in range(1, ng):
+            every = every + um[step, d]
+        w = every[depth : 2 * depth] if step == 0 else wbuf[...]
+        force = every[2 * depth : 2 * depth + 1] * (w - every[0:depth] / FOOT)
+        wbuf[...] = w - pier_gain * force
+        spread = (force[:, None, :] * in_rows[None]).reshape(depth * side, LANES)
+        pushed = jnp.dot(
+            spread, in_cols, precision=lax.Precision.HIGHEST, preferred_element_type=jnp.float32
+        )
+        acc[2] = acc[2] + soil_gain * pushed.reshape(depth, side, line)
+        start_all(there, step, 2)
+
+        for f in range(3):
+            wait_got(there, step, f)
+            if step > 0:
+                wait_sent(back, step - 1, f)
+            full = jnp.concatenate([pin[f, :, y, :] for y in range(ROWS)], axis=1)
+            damped = jnp.dot(
+                damp_ref[...], full, precision=lax.Precision.HIGHEST,
+                preferred_element_type=jnp.float32,
+            )
+            for y in range(ROWS):
+                pout[f, pl.ds(1, n * depth), y, :] = damped[:, y * LANES : (y + 1) * LANES]
+            start_all(back, step, f)
+        for f in range(3):
+            wait_got(back, step, f)
+            yg_send[step, f, 0] = v_ext[f, planes, ROWS + side - 1, :]
+            yg_send[step, f, 1] = v_ext[f, planes, ROWS, :]
+
+            @pl.when(has_next)
+            def _(f=f):
+                y_speed(step, f, 0).start()
+
+            @pl.when(has_last)
+            def _(f=f):
+                y_speed(step, f, 1).start()
+            if step == STEPS - 1:
+                pltpu.make_async_copy(
+                    v_ext.at[f, pl.ds(1, depth), inner, :], v_out.at[f], o_sem.at[f]
+                ).start()
+        if step == STEPS - 1:
+            for f in range(3):
+                pltpu.make_async_copy(
+                    v_ext.at[f, pl.ds(1, depth), inner, :], v_out.at[f], o_sem.at[f]
+                ).wait()
+        for f in range(3):
+            @pl.when(has_last)
+            def _(f=f):
+                y_speed(step, f, 0).wait_recv()
+                v_ext[f, planes, ROWS - 1, :] = yg_recv[step, f, 0]
+                y_speed(step, f, 1).wait_send()
+
+            @pl.when(has_next)
+            def _(f=f):
+                y_speed(step, f, 1).wait_recv()
+                v_ext[f, planes, ROWS + side, :] = yg_recv[step, f, 1]
+                y_speed(step, f, 0).wait_send()
+
+        if step < STEPS - 1:
+            def stress_wide(i, carry):
+                normals(i, 0, ROWS + side)
+                shears(i + 1, ROWS, ROWS + side)
+                return carry
+
+            lax.fori_loop(0, depth + 1, stress_wide, 0)
+
+            @pl.when(g == 0)
+            def _():
+                s_ext[1, planes, ROWS - 1, :] = jnp.zeros((depth + 2, line), jnp.float32)
+
+            @pl.when(g == ng - 1)
+            def _():
+                s_ext[3, planes, ROWS + side, :] = jnp.zeros((depth + 2, line), jnp.float32)
+                s_ext[5, planes, ROWS + side, :] = jnp.zeros((depth + 2, line), jnp.float32)
+        else:
+            def stress_last(i, carry):
+                normals(i + 1, ROWS, side)
+                shears(i + 1, ROWS, side)
+                return carry
+
+            lax.fori_loop(0, depth, stress_last, 0)
+
+    outs = [
+        pltpu.make_async_copy(
+            s_ext.at[f, pl.ds(1, depth), inner, :], s_out.at[f], o_sem.at[3 + f]
+        )
+        for f in range(6)
+    ]
+    for copy in outs:
+        copy.start()
+    w_out[...] = wbuf[...]
+    for f in range(3):
+        wait_sent(there, STEPS - 1, f)
+        wait_sent(back, STEPS - 1, f)
+    for copy in outs:
+        copy.wait()
+
+
+def fused_body(
+    n, ng, velocity, stress, pier_velocity, buoyancy, layer, lame_table, shear_table, relax_table,
+    impedance, footprint, damp_inverse,
+):
+    depth, side, line = buoyancy.shape
+    own = pier_velocity.shape[1]
+    piers = footprint.shape[0]
+    g = lax.axis_index("gy")
+    tables = jnp.stack([lame_table, shear_table, relax_table])
+    onehot = layer[:, None] == jnp.arange(lame_table.shape[0], dtype=jnp.int32)[None, :]
+    values = jnp.sum(jnp.where(onehot[None], tables[:, None, :], 0.0), axis=2)
+    coef = jnp.broadcast_to(values[:, :, None, None], (3, depth, ROWS, LANES))
+    lane = jnp.arange(LANES, dtype=jnp.int32)
+    w_all = lax.dynamic_update_slice(
+        jnp.zeros((depth, LANES), jnp.float32), pier_velocity, (0, g * own)
+    )
+    imp = lax.dynamic_update_slice(
+        jnp.zeros((ROWS, LANES), jnp.float32),
+        jnp.broadcast_to(impedance[None, :], (ROWS, own)), (0, g * own)
+    )
+    corner = jnp.pad(footprint[:, 0], (0, LANES - piers), constant_values=-line * 64)
+    rows = jnp.broadcast_to((corner // line)[None, :], (ROWS, LANES))
+    cols = jnp.where(lane < piers, corner % line, -64)
+    cols = jnp.broadcast_to(cols[:, None], (LANES, LANES))
+    f32 = jnp.float32
+    hbm = pl.BlockSpec(memory_space=pl.ANY)
+    vmem = pl.BlockSpec(memory_space=pltpu.VMEM)
+    dma = pltpu.SemaphoreType.DMA
+    tall = side + 2 * ROWS
+    stage = 2 * depth + ROWS
+    v, s, w = pl.pallas_call(
+        functools.partial(fused, n, ng),
+        out_shape=(
+            jax.ShapeDtypeStruct(velocity.shape, f32),
+            jax.ShapeDtypeStruct(stress.shape, f32),
+            jax.ShapeDtypeStruct((depth, LANES), f32),
+        ),
+        in_specs=[hbm] * 4 + [vmem] * 5,
+        out_specs=(hbm, hbm, vmem),
+        scratch_shapes=[
+            pltpu.VMEM((3, depth + 2, tall, line), f32),
+            pltpu.VMEM((6, depth + 2, tall, line), f32),
+            pltpu.VMEM((depth, side, line), f32),
+            pltpu.VMEM((3, depth + 2, ROWS, LANES), f32),
+            pltpu.VMEM((3, depth, side, line), f32),
+            pltpu.VMEM((3, n * depth, ROWS, LANES), f32),
+            pltpu.VMEM((3, n * depth + 2, ROWS, LANES), f32),
+            pltpu.VMEM((STEPS, ng, stage, LANES), f32),
+            pltpu.VMEM((depth, LANES), f32),
+            pltpu.VMEM((3, depth, line), f32),
+            pltpu.VMEM((3, depth, line), f32),
+            pltpu.VMEM((STEPS, 3, 2, depth + 2, line), f32),
+            pltpu.VMEM((STEPS, 3, 2, depth + 2, line), f32),
+            dma((11,)), dma((3,)), dma((3,)), dma((2,)), dma((2,)), dma((3,)), dma((3,)),
+            dma((STEPS, 3, n)), dma((STEPS, 3, n)), dma((STEPS, 3, n)), dma((STEPS, 3, n)),
+            dma((STEPS, ng)), dma((STEPS, ng)), dma((STEPS, 3, 2)), dma((STEPS, 3, 2)),
+            dma((9,)),
+        ],
+        compiler_params=pltpu.CompilerParams(
+            collective_id=0, has_side_effects=True, vmem_limit_bytes=48 * 1024 * 1024
+        ),
+    )(velocity, stress, buoyancy, coef, w_all, imp, rows, cols, damp_inverse)
+    return v, s, lax.dynamic_slice(w, (0, g * own), (depth, own))
+
+
+def whole_tiles(mesh, velocity, pier_velocity):
+    n, ng = mesh.shape["gx"], mesh.shape["gy"]
+    depth, side, line = velocity.shape[1] // n, velocity.shape[2] // ng, velocity.shape[3]
+    return (
+        line % LANES == 0
+        and side % ROWS == 0
+        and depth % ROWS == 0
+        and (side // ROWS) * (line // LANES) == n
+        and pier_velocity.shape[1] <= LANES
+    )
+
+
 def solution(mesh):
     placed = (
         P(None, "gx", "gy", None),
@@ -182,10 +661,22 @@
         P(),
         P(),
     )
-    return jax.shard_map(
-        body,
-        mesh=mesh,
-        in_specs=placed,
-        out_specs=(P(None, "gx", "gy", None), P(None, "gx", "gy", None), P("gx", "gy")),
-        check_vma=False,
-    )
+
+    def run(*args):
+        n, ng = mesh.shape["gx"], mesh.shape["gy"]
+        if whole_tiles(mesh, args[0], args[2]):
+            part = functools.partial(fused_body, n, ng)
+        else:
+            part = body
+        return mapped(part)(*args)
+
+    def mapped(part):
+        return jax.shard_map(
+            part,
+            mesh=mesh,
+            in_specs=placed,
+            out_specs=(P(None, "gx", "gy", None), P(None, "gx", "gy", None), P("gx", "gy")),
+            check_vma=False,
+        )
+
+    return run

time: 505 us -> 119 us (0.24); the launches traced: 497 us -> 118 us
  local copies, waits for them, and re-layouts: 145 us -> 10.8 us
  blocking collectives: 122 us -> 0 us
  Pallas kernels: 0 us -> 106 us
  waiting for transfers between devices: 96.1 us -> 0 us
  other arithmetic: 70.7 us -> 1.47 us
  starting transfers between devices: 31.3 us -> 0 us
  matrix products: 17.4 us -> 0 us
  between operations: 15 us -> 0.69 us
    pallas_call x0 -> x1, Pallas kernels: none -> 106 us  [fused_body(): pl.pallas_call(functools.partial(fused, n, ng), out_shape=(jax.ShapeDtype...]
    all_to_all x4 -> x0, blocking collectives: 98.2 us -> none  [the longest x2 49.2 us: damp_columns(): lax.all_to_all(velocity, 'gx', split_axis=3, concat_axis=1, tiled=True)]
    all_gather x2 -> x0, waiting for transfers between devices: 70.5 us -> none  [body(): piece = lax.all_gather(velocity[2], 'gy', axis=1, tiled=True)]
    unnamed x88 -> x12, local copies, waits for them, and re-layouts: 65.1 us -> 8.82 us
    ppermute x16 -> x0, starting transfers between devices: 30.7 us -> none  [the longest x8 19.7 us: extended(): lax.ppermute(tail, axis, [(i, (i + 1) % count) for i in range(ends)])]
    all_to_all x8 -> x0, local copies, waits for them, and re-layouts: 30.7 us -> none  [the longest x3 16.8 us: damp_columns(): lax.all_to_all(velocity, 'gx', split_axis=3, concat_axis=1, tiled=True)]
    ppermute x16 -> x0, waiting for transfers between devices: 25.6 us -> none  [the longest x8 22 us: extended(): lax.ppermute(head, axis, [((i + 1) % count, i) for i in range(ends)])]
    all_gather x2 -> x0, blocking collectives: 23.8 us -> none  [body(): all_force = lax.all_gather(force, 'gy', axis=1, tiled=True)]
  transfers between devices with their start and end apart: 18 -> 0, of which waited for: 13 -> 0; matrix products, arithmetic and copies ran while one was open for 8% -> 0% of each run, Pallas kernels for 0% -> 0%
where the time goes in v1:
time: 119 us; the launch traced here: 118 us
  Pallas kernels  106 us (89%)
  local copies, waits for them, and re-layouts  10.8 us (9%)
  other arithmetic  1.47 us (1%)
    pallas_call x1, Pallas kernels, fused_body(): pl.pallas_call(functools.partial(fused, n, ng), out_shape=(jax.ShapeDtype...  106 us
    unnamed x12, local copies, waits for them, and re-layouts  8.82 us

profile of v1, /device:TPU:0, one launch (start us, length us, event | category | flops | bytes accessed | tf_op | source)
XLA Modules:
  0.0 118.5 jit_solution(4926463502089377045)
XLA Ops:
  0.6 0.8 slice_reduce_fusion
  1.4 0.7 iota_compare_fusion
  2.1 0.7 pad_maximum_fusion
  2.8 0.1 select_reduce_fusion
  2.9 0.7 broadcast_in_dim.64
  3.6 0.1 dynamic_update_slice.7.imp_ref
  3.7 0.8 copy.18
  4.4 0.1 dynamic_update_slice.6.w_ref
  4.6 0.1 broadcast_in_dim.67.col_ref
  4.6 0.1 broadcast_in_dim.61.coef_hbm
  4.8 0.0 copy-start
  4.8 1.4 %copy-done = f32[3,16,16,512]{3,2,1,0:T(8,128)S(1)} copy-done((f32[3,16,16,512]{3,2,1,0:T(8,128)S(1)}, f32[3,16,16,512]{3,2,1,0:T(8,128)}, u32[]{:S(2)}) %copy-start) | copy-done | bytes 1572888
  6.2 0.0 copy-start.1
  6.2 1.0 copy-done.1
  7.2 0.0 copy-start.2
  7.2 0.8 copy-done.2
  8.1 105.5 %shard_map.130 = (f32[3,16,16,512]{3,2,1,0:T(8,128)S(1)}, f32[6,16,16,512]{3,2,1,0:T(8,128)}, f32[16,128]{1,0:T(8,128)S(1)}) custom-call(f32[3,16,16,512]{3,2,1,0:T(8,128)S(1)} %copy-done, f32[6,16,16,512]{3,2,1,0:T(8,128)} %s_hbm.1, f32[16,16,512]{2,1,0:T(8,128)S(1)} %copy-done.1, f32[3,16,8,128]{3,2,1,0:T(8,128)S(1)} %broadcast_in_dim.61.coef_hbm, ...), custom_call_target="tpu_custom_call" | custom-call | tf_op jit(solution)/shard_map/pallas_call | solution.py:603
  113.6 0.1 constant_dynamic-slice_fusion
  113.7 0.7 copy.19
  114.3 0.0 copy-start.3
  114.3 1.1 copy.24
  115.5 1.3 %copy-done.3 = f32[6,16,16,512]{3,2,1,0:T(8,128)S(1)} copy-done((f32[6,16,16,512]{3,2,1,0:T(8,128)S(1)}, f32[6,16,16,512]{3,2,1,0:T(8,128)}, u32[]{:S(2)}) %copy-start.3) | copy-done | bytes 3145752
  116.8 1.7 %copy.25 = f32[6,16,16,512]{3,2,1,0:T(8,128)} copy(f32[6,16,16,512]{3,2,1,0:T(8,128)S(1)} %copy-done.3) | data formatting | bytes 6291456
  (5 shorter events, 0.0 us)
Async XLA Ops:
  4.8 1.4 %copy-start = (f32[3,16,16,512]{3,2,1,0:T(8,128)S(1)}, f32[3,16,16,512]{3,2,1,0:T(8,128)}, u32[]{:S(2)}) copy-start(f32[3,16,16,512]{3,2,1,0:T(8,128)} %v_hbm.1) | copy-start | bytes 4718596
  6.2 1.0 copy-start.1
  7.2 0.8 copy-start.2
  114.3 2.5 %copy-start.3 = (f32[6,16,16,512]{3,2,1,0:T(8,128)S(1)}, f32[6,16,16,512]{3,2,1,0:T(8,128)}, u32[]{:S(2)}) copy-start(f32[6,16,16,512]{3,2,1,0:T(8,128)} %get-tuple-element.24) | copy-start | bytes 9437188

commit v2 on v1

--- a/solution.py
+++ b/solution.py
@@ -385,15 +385,20 @@
                 modulus * own + lame * others
             )
 
-    def shears(k, begin, rows):
+    def shears(k, begin, rows, which):
         at = functools.partial(cells, begin=begin, rows=rows)
-        shear, relax = wide(1, k, rows), wide(2, k, rows)
-        shear = grid_ratio * shear
-        vx, vy, vz = at(v_ext, 0, k), at(v_ext, 1, k), at(v_ext, 2, k)
-        xy = (vx - at(v_ext, 0, k, -1)) + (vy - shift_x(vy, False))
-        xz = (vx - at(v_ext, 0, k - 1)) + (vz - shift_x(vz, False))
-        yz = (vy - at(v_ext, 1, k - 1)) + (vz - at(v_ext, 2, k, -1))
-        for f, strain in ((3, xy), (4, xz), (5, yz)):
+        shear, relax = grid_ratio * wide(1, k, rows), wide(2, k, rows)
+        for f in which:
+            if f == 3:
+                vy = at(v_ext, 1, k)
+                strain = (at(v_ext, 0, k) - at(v_ext, 0, k, -1)) + (vy - shift_x(vy, False))
+            elif f == 4:
+                vz = at(v_ext, 2, k)
+                strain = (at(v_ext, 0, k) - at(v_ext, 0, k - 1)) + (vz - shift_x(vz, False))
+            else:
+                strain = (at(v_ext, 1, k) - at(v_ext, 1, k - 1)) + (
+                    at(v_ext, 2, k) - at(v_ext, 2, k, -1)
+                )
             s_ext[f, k, pl.ds(begin, rows), :] = relax * at(s_ext, f, k) + shear * strain
 
     def there(step, f, d):
@@ -450,10 +455,62 @@
     has_next, has_last = g < ng - 1, g > 0
     planes = pl.ds(0, depth + 2)
 
+    def stress_xy():
+        def at(i, carry):
+            shears(i + 1, ROWS, ROWS + side, (3,))
+            return carry
+
+        lax.fori_loop(0, depth, at, 0)
+
+        @pl.when(g == ng - 1)
+        def _():
+            s_ext[3, planes, ROWS + side, :] = jnp.zeros((depth + 2, line), jnp.float32)
+
+    def stress_xz():
+        def at(i, carry):
+            normals(i, 0, ROWS + side)
+            shears(i + 1, ROWS, side, (4,))
+            return carry
+
+        lax.fori_loop(0, depth + 1, at, 0)
+
+        @pl.when(g == 0)
+        def _():
+            s_ext[1, planes, ROWS - 1, :] = jnp.zeros((depth + 2, line), jnp.float32)
+
+    def stress_yz():
+        def at(i, carry):
+            shears(i + 1, ROWS, ROWS + side, (5,))
+            return carry
+
+        lax.fori_loop(0, depth + 1, at, 0)
+
+        @pl.when(g == ng - 1)
+        def _():
+            s_ext[5, planes, ROWS + side, :] = jnp.zeros((depth + 2, line), jnp.float32)
+
+    def v_copy(f):
+        return pltpu.make_async_copy(
+            v_ext.at[f, pl.ds(1, depth), inner, :], v_out.at[f], o_sem.at[f]
+        )
+
+    def out_copy(f):
+        return pltpu.make_async_copy(
+            s_ext.at[f, pl.ds(1, depth), inner, :], s_out.at[f], o_sem.at[3 + f]
+        )
+
     for step in range(STEPS):
         if step > 0:
             for f in range(3):
                 wait_sent(there, step - 1, f)
+        if step > 0:
+            stress_xz()
+        lax.fori_loop(0, depth, speed_x, 0)
+        start_all(there, step, 0)
+        if step > 0:
+            stress_yz()
+        lax.fori_loop(0, depth, speed_y, 0)
+        start_all(there, step, 1)
         lax.fori_loop(0, depth, speed_z, 0)
         flat = acc[2].reshape(depth * side, line)
         part = lax.dot_general(
@@ -465,10 +522,6 @@
         um[step, 0, pl.ds(2 * depth, ROWS), :] = imp_ref[...]
         for d in range(1, ng):
             share(step, d).start()
-        lax.fori_loop(0, depth, speed_x, 0)
-        start_all(there, step, 0)
-        lax.fori_loop(0, depth, speed_y, 0)
-        start_all(there, step, 1)
         for d in range(1, ng):
             share(step, d).wait()
         every = um[step, 0]
@@ -496,78 +549,74 @@
             for y in range(ROWS):
                 pout[f, pl.ds(1, n * depth), y, :] = damped[:, y * LANES : (y + 1) * LANES]
             start_all(back, step, f)
-        for f in range(3):
+        def arrive(f, step=step):
             wait_got(back, step, f)
             yg_send[step, f, 0] = v_ext[f, planes, ROWS + side - 1, :]
             yg_send[step, f, 1] = v_ext[f, planes, ROWS, :]
 
             @pl.when(has_next)
-            def _(f=f):
+            def _():
                 y_speed(step, f, 0).start()
 
             @pl.when(has_last)
-            def _(f=f):
+            def _():
                 y_speed(step, f, 1).start()
             if step == STEPS - 1:
-                pltpu.make_async_copy(
-                    v_ext.at[f, pl.ds(1, depth), inner, :], v_out.at[f], o_sem.at[f]
-                ).start()
-        if step == STEPS - 1:
-            for f in range(3):
-                pltpu.make_async_copy(
-                    v_ext.at[f, pl.ds(1, depth), inner, :], v_out.at[f], o_sem.at[f]
-                ).wait()
-        for f in range(3):
+                v_copy(f).start()
+
+        def edges(f, step=step):
             @pl.when(has_last)
-            def _(f=f):
+            def _():
                 y_speed(step, f, 0).wait_recv()
                 v_ext[f, planes, ROWS - 1, :] = yg_recv[step, f, 0]
                 y_speed(step, f, 1).wait_send()
 
             @pl.when(has_next)
-            def _(f=f):
+            def _():
                 y_speed(step, f, 1).wait_recv()
                 v_ext[f, planes, ROWS + side, :] = yg_recv[step, f, 1]
                 y_speed(step, f, 0).wait_send()
 
+        arrive(0)
+        arrive(1)
+        edges(0)
+        edges(1)
         if step < STEPS - 1:
-            def stress_wide(i, carry):
-                normals(i, 0, ROWS + side)
-                shears(i + 1, ROWS, ROWS + side)
+            stress_xy()
+            arrive(2)
+            edges(2)
+        else:
+            def last_xy(i, carry):
+                shears(i + 1, ROWS, side, (3,))
                 return carry
 
-            lax.fori_loop(0, depth + 1, stress_wide, 0)
-
-            @pl.when(g == 0)
-            def _():
-                s_ext[1, planes, ROWS - 1, :] = jnp.zeros((depth + 2, line), jnp.float32)
-
-            @pl.when(g == ng - 1)
-            def _():
-                s_ext[3, planes, ROWS + side, :] = jnp.zeros((depth + 2, line), jnp.float32)
-                s_ext[5, planes, ROWS + side, :] = jnp.zeros((depth + 2, line), jnp.float32)
-        else:
-            def stress_last(i, carry):
+            def last_shears(i, carry):
+                shears(i + 1, ROWS, side, (4, 5))
+                return carry
+
+            def last_normals(i, carry):
                 normals(i + 1, ROWS, side)
-                shears(i + 1, ROWS, side)
                 return carry
 
-            lax.fori_loop(0, depth, stress_last, 0)
-
-    outs = [
-        pltpu.make_async_copy(
-            s_ext.at[f, pl.ds(1, depth), inner, :], s_out.at[f], o_sem.at[3 + f]
-        )
-        for f in range(6)
-    ]
-    for copy in outs:
-        copy.start()
+            lax.fori_loop(0, depth, last_xy, 0)
+            out_copy(3).start()
+            arrive(2)
+            edges(2)
+            lax.fori_loop(0, depth, last_shears, 0)
+            out_copy(4).start()
+            out_copy(5).start()
+            lax.fori_loop(0, depth, last_normals, 0)
+            for f in range(3):
+                out_copy(f).start()
+
     w_out[...] = wbuf[...]
     for f in range(3):
         wait_sent(there, STEPS - 1, f)
         wait_sent(back, STEPS - 1, f)
-    for copy in outs:
-        copy.wait()
+    for f in range(3):
+        v_copy(f).wait()
+    for f in range(6):
+        out_copy(f).wait()
 
 
 def fused_body(
@@ -629,7 +678,7 @@
             dma((9,)),
         ],
         compiler_params=pltpu.CompilerParams(
-            collective_id=0, has_side_effects=True, vmem_limit_bytes=48 * 1024 * 1024
+            collective_id=0, has_side_effects=True, vmem_limit_bytes=60 * 1024 * 1024
         ),
     )(velocity, stress, buoyancy, coef, w_all, imp, rows, cols, damp_inverse)
     return v, s, lax.dynamic_slice(w, (0, g * own), (depth, own))

time: 119 us -> 116 us (0.975)
  Pallas kernels: 106 us -> 103 us
    unnamed x12 -> x10, local copies, waits for them, and re-layouts: 8.82 us -> 5.86 us
    pallas_call x1, Pallas kernels: 106 us -> 103 us  [fused_body(): pl.pallas_call(functools.partial(fused, n, ng), out_shape=(jax.ShapeDtype...]
where the time goes in v2:
time: 116 us; the launch traced here: 115 us
  Pallas kernels  103 us (89%)
  local copies, waits for them, and re-layouts  10.6 us (9%)
  other arithmetic  1.47 us (1%)
    pallas_call x1, Pallas kernels, fused_body(): pl.pallas_call(functools.partial(fused, n, ng), out_shape=(jax.ShapeDtype...  103 us
    unnamed x10, local copies, waits for them, and re-layouts  5.86 us

profile of v2, /device:TPU:0, one launch (start us, length us, event | category | flops | bytes accessed | tf_op | source)
XLA Modules:
  0.0 115.3 jit_solution(2522868787606901040)
XLA Ops:
  0.6 0.8 slice_reduce_fusion
  1.4 0.7 iota_compare_fusion
  2.1 0.7 pad_maximum_fusion
  2.8 0.1 select_reduce_fusion
  2.9 0.6 broadcast_in_dim.65.row_ref
  3.5 0.7 broadcast_in_dim.64
  4.2 0.1 dynamic_update_slice.7.imp_ref
  4.3 0.0 copy-start.2
  4.3 0.8 copy.18
  5.0 0.1 dynamic_update_slice.6.w_ref
  5.2 0.0 copy-start.1
  5.2 0.7 broadcast_in_dim.67.col_ref
  5.9 0.8 broadcast_in_dim.61.coef_hbm
  6.7 0.0 copy-done.2
  6.7 0.0 copy-done.1
  6.7 102.6 %shard_map.130 = (f32[3,16,16,512]{3,2,1,0:T(8,128)}, f32[6,16,16,512]{3,2,1,0:T(8,128)}, f32[16,128]{1,0:T(8,128)}) custom-call(f32[3,16,16,512]{3,2,1,0:T(8,128)} %v_hbm.1, f32[6,16,16,512]{3,2,1,0:T(8,128)} %s_hbm.1, f32[16,16,512]{2,1,0:T(8,128)} %b_hbm.1, f32[3,16,8,128]{3,2,1,0:T(8,128)} %broadcast_in_dim.61.coef_hbm, f32[16,128]{1,0:T(8,128)} %copy-done.1, ...), custom_call_target="tpu_custom_call" | custom-call | tf_op jit(solution)/shard_map/pallas_call | solution.py:652
  109.3 0.0 copy-start
  109.3 0.9 constant_dynamic-slice_fusion
  110.2 0.7 copy.19
  110.9 2.8 %copy.24 = f32[3,16,16,512]{3,2,1,0:T(8,128)} copy(f32[3,16,16,512]{3,2,1,0:T(8,128)} %get-tuple-element.23) | data formatting | bytes 3145728
  113.7 0.0 copy-done
  113.7 1.7 %copy.25 = f32[6,16,16,512]{3,2,1,0:T(8,128)} copy(f32[6,16,16,512]{3,2,1,0:T(8,128)S(1)} %copy-done) | data formatting | bytes 6291456
  (4 shorter events, 0.0 us)
Async XLA Ops:
  4.3 2.4 %copy-start.2 = (f32[8,128]{1,0:T(8,128)}, f32[8,128]{1,0:T(8,128)S(1)}, u32[]{:S(2)}) copy-start(f32[8,128]{1,0:T(8,128)S(1)} %dynamic_update_slice.7.imp_ref) | copy-start | bytes 12292
  5.2 1.5 %copy-start.1 = (f32[16,128]{1,0:T(8,128)}, f32[16,128]{1,0:T(8,128)S(1)}, u32[]{:S(2)}) copy-start(f32[16,128]{1,0:T(8,128)S(1)} %dynamic_update_slice.6.w_ref) | copy-start | bytes 24580
  109.3 4.4 %copy-start = (f32[6,16,16,512]{3,2,1,0:T(8,128)S(1)}, f32[6,16,16,512]{3,2,1,0:T(8,128)}, u32[]{:S(2)}) copy-start(f32[6,16,16,512]{3,2,1,0:T(8,128)} %get-tuple-element.24) | copy-start | bytes 9437188

commit v3 on v2

--- a/solution.py
+++ b/solution.py
@@ -188,7 +188,7 @@
 
 
 def fused(
-    n, ng, v_hbm, s_hbm, b_hbm, coef_hbm, w_ref, imp_ref, row_ref, col_ref, damp_ref,
+    n, ng, v_hbm, s_hbm, b_hbm, layer_ref, lame_ref, shear_ref, relax_ref, w_ref, imp_ref, row_ref, col_ref, damp_ref,
     v_out, s_out, w_out,
     v_ext, s_ext, buoy, coef, acc, pin, pout, um, wbuf, sg_send, sg_recv, yg_send, yg_recv,
     load_sem, zs_send, zs_recv, cf_send, cf_recv, ys_send, ys_recv,
@@ -216,7 +216,6 @@
         loads[("v", f)] = pltpu.make_async_copy(
             v_hbm.at[f], v_ext.at[f, pl.ds(1, depth), inner, :], load_sem.at[7 + f]
         )
-    loads["c"] = pltpu.make_async_copy(coef_hbm, coef.at[:, pl.ds(1, depth)], load_sem.at[10])
     for copy in loads.values():
         copy.start()
 
@@ -228,12 +227,15 @@
     def clear(k, carry):
         for f, way in Y_GHOSTS:
             s_ext[f, k, pl.ds(0 if way < 0 else ROWS + side, ROWS), :] = edge
-        for f in range(3):
+        for f in range(3 * STEPS):
             v_ext[f, k, pl.ds(0, ROWS), :] = edge
             v_ext[f, k, pl.ds(ROWS + side, ROWS), :] = edge
         return carry
 
     lax.fori_loop(0, depth + 2, clear, 0)
+    for k in range(depth):
+        for c, table in enumerate((lame_ref, shear_ref, relax_ref)):
+            coef[c, k + 1] = jnp.full((ROWS, LANES), table[layer_ref[k]], jnp.float32)
     for c in range(3):
         coef[c, 0] = jnp.zeros((ROWS, LANES), jnp.float32)
         coef[c, depth + 1] = jnp.zeros((ROWS, LANES), jnp.float32)
@@ -265,7 +267,7 @@
     def c_copy(way):
         i = (way + 1) // 2
         return pltpu.make_async_remote_copy(
-            src_ref=coef_hbm.at[:, depth - 1 if way < 0 else 0],
+            src_ref=coef.at[:, depth if way < 0 else 1],
             dst_ref=coef.at[:, 0 if way < 0 else depth + 1],
             send_sem=cf_send.at[i],
             recv_sem=cf_recv.at[i],
@@ -344,12 +346,14 @@
     def cells(ref, f, k, shift=0, begin=ROWS, rows=None):
         return ref[f, k, pl.ds(begin + shift, side if rows is None else rows), :]
 
+    base = [0]
+
     def speed_x(i, carry):
         k = i + 1
         xx, xy, xz = cells(s_ext, 0, k), cells(s_ext, 3, k), cells(s_ext, 4, k)
         total = (xx - shift_x(xx, False)) + (cells(s_ext, 3, k, 1) - xy)
         total = total + (cells(s_ext, 4, k + 1) - xz)
-        acc[0, i] = cells(v_ext, 0, k) + (grid_ratio * buoy[i]) * total
+        acc[0, i] = cells(v_ext, base[0] + 0, k) + (grid_ratio * buoy[i]) * total
         return carry
 
     def speed_y(i, carry):
@@ -357,7 +361,7 @@
         xy, yy, yz = cells(s_ext, 3, k), cells(s_ext, 1, k), cells(s_ext, 5, k)
         total = (shift_x(xy, True) - xy) + (yy - cells(s_ext, 1, k, -1))
         total = total + (cells(s_ext, 5, k + 1) - yz)
-        acc[1, i] = cells(v_ext, 1, k) + (grid_ratio * buoy[i]) * total
+        acc[1, i] = cells(v_ext, base[0] + 1, k) + (grid_ratio * buoy[i]) * total
         return carry
 
     def speed_z(i, carry):
@@ -365,22 +369,23 @@
         xz, yz, zz = cells(s_ext, 4, k), cells(s_ext, 5, k), cells(s_ext, 2, k)
         total = (shift_x(xz, True) - xz) + (cells(s_ext, 5, k, 1) - yz)
         total = total + (zz - cells(s_ext, 2, k - 1))
-        acc[2, i] = cells(v_ext, 2, k) + (grid_ratio * buoy[i]) * total
+        acc[2, i] = cells(v_ext, base[0] + 2, k) + (grid_ratio * buoy[i]) * total
         return carry
 
     def wide(c, k, rows):
         tile = jnp.concatenate([coef[c, k]] * tiles, axis=1)
         return jnp.concatenate([tile] * (rows // ROWS), axis=0)
 
-    def normals(k, begin, rows):
+    def normals(k, begin, rows, which=(0, 1, 2)):
         at = functools.partial(cells, begin=begin, rows=rows)
         lame, shear, relax = (wide(c, k, rows) for c in range(3))
-        vx, vy, vz = at(v_ext, 0, k), at(v_ext, 1, k), at(v_ext, 2, k)
+        vx, vy, vz = at(v_ext, base[0] + 0, k), at(v_ext, base[0] + 1, k), at(v_ext, base[0] + 2, k)
         ex = shift_x(vx, True) - vx
-        ey = at(v_ext, 1, k, 1) - vy
-        ez = at(v_ext, 2, k + 1) - vz
+        ey = at(v_ext, base[0] + 1, k, 1) - vy
+        ez = at(v_ext, base[0] + 2, k + 1) - vz
         modulus = lame + 2.0 * shear
-        for f, own, others in ((0, ex, ey + ez), (1, ey, ex + ez), (2, ez, ex + ey)):
+        for f in which:
+            own, others = ((ex, ey + ez), (ey, ex + ez), (ez, ex + ey))[f]
             s_ext[f, k, pl.ds(begin, rows), :] = relax * at(s_ext, f, k) + grid_ratio * (
                 modulus * own + lame * others
             )
@@ -390,14 +395,14 @@
         shear, relax = grid_ratio * wide(1, k, rows), wide(2, k, rows)
         for f in which:
             if f == 3:
-                vy = at(v_ext, 1, k)
-                strain = (at(v_ext, 0, k) - at(v_ext, 0, k, -1)) + (vy - shift_x(vy, False))
+                vy = at(v_ext, base[0] + 1, k)
+                strain = (at(v_ext, base[0] + 0, k) - at(v_ext, base[0] + 0, k, -1)) + (vy - shift_x(vy, False))
             elif f == 4:
-                vz = at(v_ext, 2, k)
-                strain = (at(v_ext, 0, k) - at(v_ext, 0, k - 1)) + (vz - shift_x(vz, False))
+                vz = at(v_ext, base[0] + 2, k)
+                strain = (at(v_ext, base[0] + 0, k) - at(v_ext, base[0] + 0, k - 1)) + (vz - shift_x(vz, False))
             else:
-                strain = (at(v_ext, 1, k) - at(v_ext, 1, k - 1)) + (
-                    at(v_ext, 2, k) - at(v_ext, 2, k, -1)
+                strain = (at(v_ext, base[0] + 1, k) - at(v_ext, base[0] + 1, k - 1)) + (
+                    at(v_ext, base[0] + 2, k) - at(v_ext, base[0] + 2, k, -1)
                 )
             s_ext[f, k, pl.ds(begin, rows), :] = relax * at(s_ext, f, k) + shear * strain
 
@@ -416,8 +421,10 @@
     def back(step, f, d):
         t = lax.rem(me + d, n)
         ys, xs = pl.ds(pl.multiple_of((me // tiles) * ROWS + ROWS, ROWS), ROWS), piece(me)[1]
-        src = pout.at[f, pl.ds(t * depth, depth + 2)]
-        dst = v_ext.at[f, :, ys, xs]
+        last = step == STEPS - 1
+        low, count = (1 if last and f == 2 else 0), depth + (1 if last else 2)
+        src = pout.at[f, pl.ds(t * depth + low, count)]
+        dst = v_ext.at[3 * step + f, pl.ds(low, count), ys, xs]
         if d == 0:
             return pltpu.make_async_copy(src, dst, r_recv.at[step, f, 0])
         return pltpu.make_async_remote_copy(
@@ -468,36 +475,74 @@
 
     def stress_xz():
         def at(i, carry):
-            normals(i, 0, ROWS + side)
+            normals(i + 1, ROWS, side, (0,))
             shears(i + 1, ROWS, side, (4,))
             return carry
 
-        lax.fori_loop(0, depth + 1, at, 0)
+        lax.fori_loop(0, depth, at, 0)
+        shears(depth + 1, ROWS, side, (4,))
+
+    def stress_yz():
+        def at(i, carry):
+            normals(i + 1, 0, ROWS + side, (1,))
+            shears(i + 1, ROWS, ROWS + side, (5,))
+            return carry
+
+        lax.fori_loop(0, depth, at, 0)
+        shears(depth + 1, ROWS, side, (5,))
 
         @pl.when(g == 0)
         def _():
             s_ext[1, planes, ROWS - 1, :] = jnp.zeros((depth + 2, line), jnp.float32)
 
-    def stress_yz():
-        def at(i, carry):
-            shears(i + 1, ROWS, ROWS + side, (5,))
-            return carry
-
-        lax.fori_loop(0, depth + 1, at, 0)
-
         @pl.when(g == ng - 1)
         def _():
             s_ext[5, planes, ROWS + side, :] = jnp.zeros((depth + 2, line), jnp.float32)
 
+    def stress_zz():
+        def at(i, carry):
+            normals(i, ROWS, side, (2,))
+            return carry
+
+        lax.fori_loop(0, depth + 1, at, 0)
+
     def v_copy(f):
         return pltpu.make_async_copy(
-            v_ext.at[f, pl.ds(1, depth), inner, :], v_out.at[f], o_sem.at[f]
+            v_ext.at[3 * (STEPS - 1) + f, pl.ds(1, depth), inner, :], v_out.at[f], o_sem.at[f]
         )
 
     def out_copy(f):
         return pltpu.make_async_copy(
             s_ext.at[f, pl.ds(1, depth), inner, :], s_out.at[f], o_sem.at[3 + f]
         )
+
+    def arrive(f, step):
+        wait_got(back, step, f)
+        yg_send[step, f, 0] = v_ext[3 * step + f, planes, ROWS + side - 1, :]
+        yg_send[step, f, 1] = v_ext[3 * step + f, planes, ROWS, :]
+
+        @pl.when(has_next)
+        def _():
+            y_speed(step, f, 0).start()
+
+        @pl.when(has_last)
+        def _():
+            y_speed(step, f, 1).start()
+        if step == STEPS - 1:
+            v_copy(f).start()
+
+    def edges(f, step):
+        @pl.when(has_last)
+        def _():
+            y_speed(step, f, 0).wait_recv()
+            v_ext[3 * step + f, planes, ROWS - 1, :] = yg_recv[step, f, 0]
+            y_speed(step, f, 1).wait_send()
+
+        @pl.when(has_next)
+        def _():
+            y_speed(step, f, 1).wait_recv()
+            v_ext[3 * step + f, planes, ROWS + side, :] = yg_recv[step, f, 1]
+            y_speed(step, f, 0).wait_send()
 
     for step in range(STEPS):
         if step > 0:
@@ -508,9 +553,12 @@
         lax.fori_loop(0, depth, speed_x, 0)
         start_all(there, step, 0)
         if step > 0:
+            edges(2, step - 1)
             stress_yz()
         lax.fori_loop(0, depth, speed_y, 0)
         start_all(there, step, 1)
+        if step > 0:
+            stress_zz()
         lax.fori_loop(0, depth, speed_z, 0)
         flat = acc[2].reshape(depth * side, line)
         part = lax.dot_general(
@@ -549,65 +597,37 @@
             for y in range(ROWS):
                 pout[f, pl.ds(1, n * depth), y, :] = damped[:, y * LANES : (y + 1) * LANES]
             start_all(back, step, f)
-        def arrive(f, step=step):
-            wait_got(back, step, f)
-            yg_send[step, f, 0] = v_ext[f, planes, ROWS + side - 1, :]
-            yg_send[step, f, 1] = v_ext[f, planes, ROWS, :]
-
-            @pl.when(has_next)
-            def _():
-                y_speed(step, f, 0).start()
-
-            @pl.when(has_last)
-            def _():
-                y_speed(step, f, 1).start()
-            if step == STEPS - 1:
-                v_copy(f).start()
-
-        def edges(f, step=step):
-            @pl.when(has_last)
-            def _():
-                y_speed(step, f, 0).wait_recv()
-                v_ext[f, planes, ROWS - 1, :] = yg_recv[step, f, 0]
-                y_speed(step, f, 1).wait_send()
-
-            @pl.when(has_next)
-            def _():
-                y_speed(step, f, 1).wait_recv()
-                v_ext[f, planes, ROWS + side, :] = yg_recv[step, f, 1]
-                y_speed(step, f, 0).wait_send()
-
-        arrive(0)
-        arrive(1)
-        edges(0)
-        edges(1)
+        base[0] = 3 * step
+        arrive(0, step)
+        arrive(1, step)
+        edges(0, step)
+        edges(1, step)
         if step < STEPS - 1:
             stress_xy()
-            arrive(2)
-            edges(2)
+            arrive(2, step)
         else:
             def last_xy(i, carry):
                 shears(i + 1, ROWS, side, (3,))
                 return carry
 
-            def last_shears(i, carry):
-                shears(i + 1, ROWS, side, (4, 5))
+            def last_rest(i, carry):
+                normals(i + 1, ROWS, side)
+                shears(i + 1, ROWS, side, (4,))
                 return carry
 
-            def last_normals(i, carry):
-                normals(i + 1, ROWS, side)
+            def last_yz(i, carry):
+                shears(i + 1, ROWS, side, (5,))
                 return carry
 
             lax.fori_loop(0, depth, last_xy, 0)
             out_copy(3).start()
-            arrive(2)
-            edges(2)
-            lax.fori_loop(0, depth, last_shears, 0)
-            out_copy(4).start()
+            arrive(2, step)
+            lax.fori_loop(0, depth, last_rest, 0)
+            for f in (0, 1, 2, 4):
+                out_copy(f).start()
+            edges(2, step)
+            lax.fori_loop(0, depth, last_yz, 0)
             out_copy(5).start()
-            lax.fori_loop(0, depth, last_normals, 0)
-            for f in range(3):
-                out_copy(f).start()
 
     w_out[...] = wbuf[...]
     for f in range(3):
@@ -627,10 +647,6 @@
     own = pier_velocity.shape[1]
     piers = footprint.shape[0]
     g = lax.axis_index("gy")
-    tables = jnp.stack([lame_table, shear_table, relax_table])
-    onehot = layer[:, None] == jnp.arange(lame_table.shape[0], dtype=jnp.int32)[None, :]
-    values = jnp.sum(jnp.where(onehot[None], tables[:, None, :], 0.0), axis=2)
-    coef = jnp.broadcast_to(values[:, :, None, None], (3, depth, ROWS, LANES))
     lane = jnp.arange(LANES, dtype=jnp.int32)
     w_all = lax.dynamic_update_slice(
         jnp.zeros((depth, LANES), jnp.float32), pier_velocity, (0, g * own)
@@ -646,6 +662,7 @@
     f32 = jnp.float32
     hbm = pl.BlockSpec(memory_space=pl.ANY)
     vmem = pl.BlockSpec(memory_space=pltpu.VMEM)
+    smem = pl.BlockSpec(memory_space=pltpu.SMEM)
     dma = pltpu.SemaphoreType.DMA
     tall = side + 2 * ROWS
     stage = 2 * depth + ROWS
@@ -656,10 +673,10 @@
             jax.ShapeDtypeStruct(stress.shape, f32),
             jax.ShapeDtypeStruct((depth, LANES), f32),
         ),
-        in_specs=[hbm] * 4 + [vmem] * 5,
+        in_specs=[hbm] * 3 + [smem] * 4 + [vmem] * 5,
         out_specs=(hbm, hbm, vmem),
         scratch_shapes=[
-            pltpu.VMEM((3, depth + 2, tall, line), f32),
+            pltpu.VMEM((3 * STEPS, depth + 2, tall, line), f32),
             pltpu.VMEM((6, depth + 2, tall, line), f32),
             pltpu.VMEM((depth, side, line), f32),
             pltpu.VMEM((3, depth + 2, ROWS, LANES), f32),
@@ -672,7 +689,7 @@
             pltpu.VMEM((3, depth, line), f32),
             pltpu.VMEM((STEPS, 3, 2, depth + 2, line), f32),
             pltpu.VMEM((STEPS, 3, 2, depth + 2, line), f32),
-            dma((11,)), dma((3,)), dma((3,)), dma((2,)), dma((2,)), dma((3,)), dma((3,)),
+            dma((10,)), dma((3,)), dma((3,)), dma((2,)), dma((2,)), dma((3,)), dma((3,)),
             dma((STEPS, 3, n)), dma((STEPS, 3, n)), dma((STEPS, 3, n)), dma((STEPS, 3, n)),
             dma((STEPS, ng)), dma((STEPS, ng)), dma((STEPS, 3, 2)), dma((STEPS, 3, 2)),
             dma((9,)),
@@ -680,7 +697,10 @@
         compiler_params=pltpu.CompilerParams(
             collective_id=0, has_side_effects=True, vmem_limit_bytes=60 * 1024 * 1024
         ),
-    )(velocity, stress, buoyancy, coef, w_all, imp, rows, cols, damp_inverse)
+    )(
+        velocity, stress, buoyancy, layer, lame_table, shear_table, relax_table,
+        w_all, imp, rows, cols, damp_inverse,
+    )
     return v, s, lax.dynamic_slice(w, (0, g * own), (depth, own))
 
 

time: 116 us -> 107 us (0.922)
  Pallas kernels: 103 us -> 96 us
  other arithmetic: 1.47 us -> 0.02 us
    pallas_call x1, Pallas kernels: 103 us -> 96 us  [fused_body(): pl.pallas_call(functools.partial(fused, n, ng), out_shape=(jax.ShapeDtype...]
where the time goes in v3:
time: 107 us; the launch traced here: 106 us
  Pallas kernels  96 us (90%)
  local copies, waits for them, and re-layouts  9.76 us (9%)
    pallas_call x1, Pallas kernels, fused_body(): pl.pallas_call(functools.partial(fused, n, ng), out_shape=(jax.ShapeDtype...  96 us
    unnamed x10, local copies, waits for them, and re-layouts  5.86 us

profile of v3, /device:TPU:0, one launch (start us, length us, event | category | flops | bytes accessed | tf_op | source)
XLA Modules:
  0.0 106.5 jit_solution(17735481067500842343)
XLA Ops:
  0.6 0.8 slice_reduce_fusion
  1.5 0.6 broadcast_in_dim.31.row_ref
  2.1 0.7 broadcast_in_dim.30
  2.7 0.1 dynamic_update_slice.7.imp_ref
  2.8 0.0 copy-start.2
  2.8 0.8 copy.16
  3.6 0.1 dynamic_update_slice.6.w_ref
  3.7 0.0 copy-start.1
  3.7 0.7 broadcast_in_dim.33.col_ref
  4.4 0.0 copy-done.2
  4.4 0.0 copy-done.1
  4.5 96.0 %shard_map.130 = (f32[3,16,16,512]{3,2,1,0:T(8,128)}, f32[6,16,16,512]{3,2,1,0:T(8,128)}, f32[16,128]{1,0:T(8,128)}) custom-call(f32[3,16,16,512]{3,2,1,0:T(8,128)} %v_hbm.1, f32[6,16,16,512]{3,2,1,0:T(8,128)} %s_hbm.1, f32[16,16,512]{2,1,0:T(8,128)} %b_hbm.1, s32[16]{0:T(128)} %layer_ref.1, f32[8]{0:T(128)} %lame_ref.1, f32[8]{0:T(128)} %shear_ref.1, ...), custom_call_target="tpu_custom_call" | custom-call | tf_op jit(solution)/shard_map/pallas_call | solution.py:669
  100.4 0.0 copy-start
  100.4 0.9 constant_dynamic-slice_fusion
  101.4 0.7 copy.17
  102.0 2.8 %copy.22 = f32[3,16,16,512]{3,2,1,0:T(8,128)} copy(f32[3,16,16,512]{3,2,1,0:T(8,128)} %get-tuple-element.20) | data formatting | bytes 3145728
  104.8 0.0 copy-done
  104.8 1.7 %copy.23 = f32[6,16,16,512]{3,2,1,0:T(8,128)} copy(f32[6,16,16,512]{3,2,1,0:T(8,128)S(1)} %copy-done) | data formatting | bytes 6291456
  (4 shorter events, 0.0 us)
Async XLA Ops:
  2.8 1.6 %copy-start.2 = (f32[8,128]{1,0:T(8,128)}, f32[8,128]{1,0:T(8,128)S(1)}, u32[]{:S(2)}) copy-start(f32[8,128]{1,0:T(8,128)S(1)} %dynamic_update_slice.7.imp_ref) | copy-start | bytes 12292
  3.7 0.7 copy-start.1
  100.4 4.4 %copy-start = (f32[6,16,16,512]{3,2,1,0:T(8,128)S(1)}, f32[6,16,16,512]{3,2,1,0:T(8,128)}, u32[]{:S(2)}) copy-start(f32[6,16,16,512]{3,2,1,0:T(8,128)} %get-tuple-element.21) | copy-start | bytes 9437188

commit v4 on v3

--- a/solution.py
+++ b/solution.py
@@ -188,7 +188,7 @@
 
 
 def fused(
-    n, ng, v_hbm, s_hbm, b_hbm, layer_ref, lame_ref, shear_ref, relax_ref, w_ref, imp_ref, row_ref, col_ref, damp_ref,
+    n, ng, v_hbm, s_hbm, b_hbm, layer_ref, lame_ref, shear_ref, relax_ref, foot_ref, w_ref, imp_ref, damp_ref,
     v_out, s_out, w_out,
     v_ext, s_ext, buoy, coef, acc, pin, pout, um, wbuf, sg_send, sg_recv, yg_send, yg_recv,
     load_sem, zs_send, zs_recv, cf_send, cf_recv, ys_send, ys_recv,
@@ -311,10 +311,16 @@
             copy.wait()
 
     ids = lax.broadcasted_iota(jnp.int32, (side, LANES), 0) + g * side
-    first = row_ref[0:1, :]
+    by_lane = lax.broadcasted_iota(jnp.int32, (side, LANES), 1)
+    by_row = lax.broadcasted_iota(jnp.int32, (LANES, LANES), 0)
+    first = jnp.full((side, LANES), -64, jnp.int32)
+    begin = jnp.full((LANES, LANES), -64, jnp.int32)
+    for p in range(foot_ref.shape[0]):
+        first = jnp.where(by_lane == p, foot_ref[p, 0] // line, first)
+        begin = jnp.where(by_row == p, foot_ref[p, 0] % line, begin)
     in_rows = jnp.where((ids >= first) & (ids < first + SIDE), 1.0, 0.0)
     across = lax.broadcasted_iota(jnp.int32, (LANES, line), 1)
-    start = jnp.concatenate([col_ref[...]] * tiles, axis=1)
+    start = jnp.concatenate([begin] * tiles, axis=1)
     in_cols = jnp.where((across >= start) & (across < start + SIDE), 1.0, 0.0)
 
     for i, (f, way) in enumerate(Z_GHOSTS):
@@ -645,9 +651,7 @@
 ):
     depth, side, line = buoyancy.shape
     own = pier_velocity.shape[1]
-    piers = footprint.shape[0]
     g = lax.axis_index("gy")
-    lane = jnp.arange(LANES, dtype=jnp.int32)
     w_all = lax.dynamic_update_slice(
         jnp.zeros((depth, LANES), jnp.float32), pier_velocity, (0, g * own)
     )
@@ -655,10 +659,6 @@
         jnp.zeros((ROWS, LANES), jnp.float32),
         jnp.broadcast_to(impedance[None, :], (ROWS, own)), (0, g * own)
     )
-    corner = jnp.pad(footprint[:, 0], (0, LANES - piers), constant_values=-line * 64)
-    rows = jnp.broadcast_to((corner // line)[None, :], (ROWS, LANES))
-    cols = jnp.where(lane < piers, corner % line, -64)
-    cols = jnp.broadcast_to(cols[:, None], (LANES, LANES))
     f32 = jnp.float32
     hbm = pl.BlockSpec(memory_space=pl.ANY)
     vmem = pl.BlockSpec(memory_space=pltpu.VMEM)
@@ -673,7 +673,7 @@
             jax.ShapeDtypeStruct(stress.shape, f32),
             jax.ShapeDtypeStruct((depth, LANES), f32),
         ),
-        in_specs=[hbm] * 3 + [smem] * 4 + [vmem] * 5,
+        in_specs=[hbm] * 3 + [smem] * 5 + [vmem] * 3,
         out_specs=(hbm, hbm, vmem),
         scratch_shapes=[
             pltpu.VMEM((3 * STEPS, depth + 2, tall, line), f32),
@@ -699,7 +699,7 @@
         ),
     )(
         velocity, stress, buoyancy, layer, lame_table, shear_table, relax_table,
-        w_all, imp, rows, cols, damp_inverse,
+        footprint, w_all, imp, damp_inverse,
     )
     return v, s, lax.dynamic_slice(w, (0, g * own), (depth, own))
 

time: 107 us -> 105 us (0.981)
  local copies, waits for them, and re-layouts: 9.76 us -> 8.24 us
    broadcast_in_dim x2 -> x0, local copies, waits for them, and re-layouts: 1.31 us -> none  [the longest x1 0.71 us: fused_body(): cols = jnp.broadcast_to(cols[:, None], (LANES, LANES))]
where the time goes in v4:
time: 105 us
  Pallas kernels  96.1 us (92%)
  local copies, waits for them, and re-layouts  8.24 us (8%)
    pallas_call x1, Pallas kernels, fused_body(): pl.pallas_call(functools.partial(fused, n, ng), out_shape=(jax.ShapeDtype...  96.1 us
    unnamed x10, local copies, waits for them, and re-layouts  6.45 us

profile of v4, /device:TPU:0, one launch (start us, length us, event | category | flops | bytes accessed | tf_op | source)
XLA Modules:
  0.0 105.1 jit_solution(16272519476949043363)
XLA Ops:
  0.6 0.7 broadcast_in_dim.14
  1.3 0.1 dynamic_update_slice.7.imp_ref
  1.4 0.0 copy-start.2
  1.4 0.8 copy.14
  2.2 0.1 dynamic_update_slice.6.w_ref
  2.3 0.0 copy-done.2
  2.3 0.0 copy-start.1
  2.3 0.6 copy-done.1
  2.9 96.1 %shard_map.130 = (f32[3,16,16,512]{3,2,1,0:T(8,128)}, f32[6,16,16,512]{3,2,1,0:T(8,128)}, f32[16,128]{1,0:T(8,128)}) custom-call(f32[3,16,16,512]{3,2,1,0:T(8,128)} %v_hbm.1, f32[6,16,16,512]{3,2,1,0:T(8,128)} %s_hbm.1, f32[16,16,512]{2,1,0:T(8,128)} %b_hbm.1, s32[16]{0:T(128)} %layer_ref.1, f32[8]{0:T(128)} %lame_ref.1, f32[8]{0:T(128)} %shear_ref.1, ...), custom_call_target="tpu_custom_call" | custom-call | tf_op jit(solution)/shard_map/pallas_call | solution.py:669
  99.1 0.0 copy-start
  99.1 0.9 constant_dynamic-slice_fusion
  100.0 0.7 copy.15
  100.6 2.8 %copy.20 = f32[3,16,16,512]{3,2,1,0:T(8,128)} copy(f32[3,16,16,512]{3,2,1,0:T(8,128)} %get-tuple-element.15) | data formatting | bytes 3145728
  103.4 0.0 copy-done
  103.4 1.7 %copy.21 = f32[6,16,16,512]{3,2,1,0:T(8,128)} copy(f32[6,16,16,512]{3,2,1,0:T(8,128)S(1)} %copy-done) | data formatting | bytes 6291456
  (2 shorter events, 0.0 us)
Async XLA Ops:
  1.4 0.9 copy-start.2
  2.3 0.6 copy-start.1
  99.1 4.4 %copy-start = (f32[6,16,16,512]{3,2,1,0:T(8,128)S(1)}, f32[6,16,16,512]{3,2,1,0:T(8,128)}, u32[]{:S(2)}) copy-start(f32[6,16,16,512]{3,2,1,0:T(8,128)} %get-tuple-element.16) | copy-start | bytes 9437188
